TPU v7x, 512 devices: a whole 4x4x16 slice. The times are simulated.
512 devices in a mesh: row: 64 (over x_lo, z, core), col: 8 (over x_hi, y).
Axes of the slice: x: 4 (x_hi: 2, x_lo: 2; x = x_hi * 2 + x_lo), y: 4, z: 16, core: 2. Of those that a mesh axis runs over, the one named last changes fastest.
Arguments:
- amplitudes: bfloat16 [1024, 160000], P(('row', 'col')), may hold values from -6 to 6
- integrals: bfloat16 [160000, 1024], P('row', 'col'), may hold values from -0.03125 to 0.03125
- occ_irreps: int32 [50], replicated, may hold values from 0 to 3
- block_sizes: int32 [4], replicated, may hold values from 1 to 160, 400 in all
Outputs:
- ladder: bfloat16 [1024, 1024], P('row', 'col')
Inputs may be any that keep to these rules, and one draw needn't show every extreme that they name: `block_sizes`: the virtual orbitals are ordered by irrep; these are the sizes of the 4 blocks, summing to 400.
All inputs are finite; a program needn't handle non-finite values.
Results may differ from a plain program's by a relative error of at most 0.003.
Values may be sent and summed in bfloat16 or wider, within the bound.
No kernel may reach another device: no remote copies, remote signals or barrier semaphores. Data moves between devices by JAX's collectives and lax.ppermute only.
A program may use at most 64 MiB of HBM per device.

v0:
```python
import jax
import jax.numpy as jnp
from jax import lax
from jax.sharding import PartitionSpec as P

OCCUPIED = 50
VIRTUAL = 400


def virtual_labels(block_sizes):
    ends = jnp.cumsum(block_sizes)
    orbital = jnp.arange(VIRTUAL, dtype=jnp.int32)
    return jnp.sum((orbital[:, None] >= ends[None, :]).astype(jnp.int32), axis=1)


def on_device(amplitudes, integrals, occ_irreps, block_sizes):
    row_count = lax.axis_size("row")
    col_count = lax.axis_size("col")
    row_index = lax.axis_index("row")
    col_index = lax.axis_index("col")
    local_pairs = amplitudes.shape[0]
    contracted = integrals.shape[0]
    columns = integrals.shape[1]
    virt_irrep = virtual_labels(block_sizes)
    virt_pair = jnp.bitwise_xor(virt_irrep[:, None], virt_irrep[None, :]).reshape(VIRTUAL * VIRTUAL)
    first_pair = (row_index * col_count + col_index) * local_pairs
    pair_ids = first_pair + jnp.arange(local_pairs, dtype=jnp.int32)
    occ_pair = jnp.bitwise_xor(occ_irreps[pair_ids // OCCUPIED], occ_irreps[pair_ids % OCCUPIED])
    masked = jnp.where(
        occ_pair[:, None] == virt_pair[None, :], amplitudes, jnp.zeros_like(amplitudes)
    )
    regrouped = lax.all_to_all(masked, "row", split_axis=1, concat_axis=0, tiled=True)
    local_irrep = lax.dynamic_slice_in_dim(virt_pair, row_index * contracted, contracted)
    out_irrep = lax.dynamic_slice_in_dim(virt_pair, col_index * columns, columns)
    kept = jnp.where(
        local_irrep[:, None] == out_irrep[None, :], integrals, jnp.zeros_like(integrals)
    )
    partial_value = jnp.dot(
        regrouped,
        lax.all_gather(kept, "col", axis=1, tiled=True),
        preferred_element_type=jnp.float32,
    )
    shaped = partial_value.reshape(row_count, local_pairs, columns * col_count)
    summed = lax.psum_scatter(shaped, "row", scatter_dimension=0, tiled=True)
    rounded = summed.reshape(local_pairs, columns * col_count).astype(jnp.bfloat16)
    return lax.all_to_all(rounded, "col", split_axis=1, concat_axis=0, tiled=True)


def solution(mesh):
    in_specs = (P(("row", "col"), None), P("row", "col"), P(), P())
    out_specs = P("row", "col")
    return jax.shard_map(
        on_device, mesh=mesh, in_specs=in_specs, out_specs=out_specs, check_vma=False
    )
```

profile of v0, /device:TPU:2, one launch (start us, length us, event | category | flops | bytes accessed | tf_op | source)
XLA Modules:
  0.0 351.5 jit_solution(17285738413955634931)
XLA Ops:
  6.5 0.0 copy-start
  6.5 0.0 copy-start.1
  6.5 0.0 all-gather.2.cloned.1.call-start
  6.5 0.9 reduce-window.8
  7.4 0.1 convert_reduce_fusion
  7.5 0.1 broadcast_xor_fusion
  7.7 0.7 xor.32
  8.4 0.1 dynamic_slice.7
  8.4 0.1 dynamic_slice.6
  8.5 2.8 compare_select_fusion.1
  11.3 0.0 all-gather.2.cloned.1.call-update
  11.4 0.0 copy-done
  11.4 0.6 gather_fusion
  12.1 0.6 gather_fusion.1
  12.7 0.0 copy-done.1
  12.7 3.0 compare_select_fusion
  15.8 1.6 all_to_all.24
  17.4 1.5 copy.14
  19.0 17.2 %all-to-all-start = ((bf16[2,64,2500]{2,0,1:T(2,128)(2,1)}), bf16[2,64,2500]{2,0,1:T(2,128)(2,1)S(1)}, u32[]{:S(2)}, u32[]{:S(2)}) async-start(bf16[2,64,2500]{2,0,1:T(2,128)(2,1)} %copy.14), calls=%async_computation | async-start | bytes 1310720 | tf_op jit(solution)/shard_map/all_to_all | solution.py:32
  36.2 1.3 dynamic-slice
  37.4 34.2 %all-to-all-done = bf16[2,64,2500]{2,0,1:T(2,128)(2,1)S(1)} async-done(((bf16[2,64,2500]{2,0,1:T(2,128)(2,1)}), bf16[2,64,2500]{2,0,1:T(2,128)(2,1)S(1)}, u32[]{:S(2)}, u32[]{:S(2)}) %all-to-all-start) | async-done | bytes 640032 | tf_op jit(solution)/shard_map/all_to_all | solution.py:32
  71.7 43.4 %all-gather.2.cloned.1.call-done = bf16[2500,1024]{1,0:T(8,128)(2,1)} async-done(((bf16[2500,128]{1,0:T(8,128)(2,1)}), bf16[2500,1024]{1,0:T(8,128)(2,1)}) %all-gather.2.cloned.1.call-update) | async-done | bytes 5120016 | tf_op jit(solution)/shard_map/all_gather | solution.py:40
  115.1 3.5 fusion
  118.6 0.4 copy.16
  119.0 214.2 %all-reduce.2 = bf16[64,2,1024]{2,1,0:T(2,128)(2,1)S(1)} all-reduce(f32[64,2,1024]{2,1,0:T(2,128)S(1)} %copy.16), channel_id=2, replica_groups=mesh['row'=64,'col'=8] {'row'}, use_global_device_ids=true, to_apply=%region_2.3.clone | all-reduce | flops 131072 | bytes 786432
  333.2 0.7 fusion.4
  333.9 10.2 %all_to_all.32 = bf16[2,8,128]{2,0,1:T(2,128)(2,1)S(1)} all-to-all(bf16[2,8,128]{2,0,1:T(2,128)(2,1)S(1)} %fusion.4), channel_id=1, replica_groups=mesh['row'=64,'col'=8] {'col'}, dimensions={1} | all-to-all | bytes 8192 | tf_op jit(solution)/shard_map/all_to_all | solution.py:46
  344.1 0.6 copy.25
  (4 shorter events, 0.0 us)
Async XLA Ops:
  6.5 4.9 %copy-start = (s32[50]{0:T(128)S(1)}, s32[50]{0:T(128)}, u32[]{:S(2)}) copy-start(s32[50]{0:T(128)} %param.6) | copy-start | bytes 604
  6.5 6.2 %copy-start.1 = (bf16[2,160000]{1,0:T(2,128)(2,1)S(1)}, bf16[2,160000]{1,0:T(2,128)(2,1)}, u32[]{:S(2)}) copy-start(bf16[2,160000]{1,0:T(2,128)(2,1)} %param.4) | copy-start | bytes 1920004
  6.5 108.5 %all-gather.2.cloned.1.call-start = ((), (), s32[]{:S(2)}) async-start(), calls=%async_computation.2 | async-start | bytes 5769216 | tf_op jit(solution)/shard_map/all_gather | solution.py:40
  19.0 52.7 %all-to-all-start = ((bf16[2,64,2500]{2,0,1:T(2,128)(2,1)}), bf16[2,64,2500]{2,0,1:T(2,128)(2,1)S(1)}, u32[]{:S(2)}, u32[]{:S(2)}) async-start(bf16[2,64,2500]{2,0,1:T(2,128)(2,1)} %copy.14), calls=%async_computation | async-start | bytes 1310720 | tf_op jit(solution)/shard_map/all_to_all | solution.py:32
Sparse Core Ops, SparseCore 0:
  11.5 103.5 all-gather.1
where the time goes:
time: 352 us
  blocking collectives  224 us (64%)
  waiting for transfers between devices  77.6 us (22%)
  starting transfers between devices  17.2 us (5%)
  between operations  13.5 us (4%)
  local copies, waits for them, and re-layouts  8.24 us (2%)
  other arithmetic  7 us (2%)
    unnamed x1, blocking collectives  214 us
    all_gather x1, waiting for transfers between devices, on_device(): lax.all_gather(kept, 'col', axis=1, tiled=True)  43.4 us
    all_to_all x1, waiting for transfers between devices, on_device(): lax.all_to_all(masked, 'row', split_axis=1, concat_axis=0, tiled=True)  34.2 us
    all_to_all x1, starting transfers between devices, on_device(): lax.all_to_all(masked, 'row', split_axis=1, concat_axis=0, tiled=True)  17.2 us
    all_to_all x1, blocking collectives, on_device(): lax.all_to_all(rounded, 'col', split_axis=1, concat_axis=0, tiled=True)  10.2 us
  transfers between devices with their start and end apart: 2, of which 2 were waited for; matrix products, arithmetic and copies ran while one was open for 2% of the time, Pallas kernels for 0%

commit v1 on v0

--- a/solution.py
+++ b/solution.py
@@ -8,7 +8,7 @@
 
 
 def virtual_labels(block_sizes):
-    ends = jnp.cumsum(block_sizes)
+    ends = jnp.sum(jnp.tril(jnp.ones((4, 4), jnp.int32)) * block_sizes[None, :], axis=1)
     orbital = jnp.arange(VIRTUAL, dtype=jnp.int32)
     return jnp.sum((orbital[:, None] >= ends[None, :]).astype(jnp.int32), axis=1)
 
@@ -40,8 +40,11 @@
         lax.all_gather(kept, "col", axis=1, tiled=True),
         preferred_element_type=jnp.float32,
     )
-    shaped = partial_value.reshape(row_count, local_pairs, columns * col_count)
-    summed = lax.psum_scatter(shaped, "row", scatter_dimension=0, tiled=True)
+    shaped = partial_value.reshape(row_count, local_pairs * columns * col_count // 128, 128)
+    pieces = lax.all_to_all(
+        shaped.astype(jnp.bfloat16), "row", split_axis=0, concat_axis=0, tiled=True
+    )
+    summed = jnp.sum(pieces.astype(jnp.float32), axis=0)
     rounded = summed.reshape(local_pairs, columns * col_count).astype(jnp.bfloat16)
     return lax.all_to_all(rounded, "col", split_axis=1, concat_axis=0, tiled=True)
 

time: 352 us -> 175 us (0.50)
  the two profiles are of different devices: /device:TPU:2 before, /device:TPU:1 now
where the time goes in v1:
time: 175 us
  blocking collectives  100 us (57%)
  waiting for transfers between devices  44.8 us (26%)
  between operations  13.5 us (8%)
  other arithmetic  7.04 us (4%)
  local copies, waits for them, and re-layouts  5.66 us (3%)
  matrix products  3.53 us (2%)
    all_to_all x1, blocking collectives, on_device(): lax.all_to_all(masked, 'row', split_axis=1, concat_axis=0, tiled=True)  53.9 us
    all_gather x1, waiting for transfers between devices, on_device(): lax.all_gather(kept, 'col', axis=1, tiled=True)  44.8 us
    all_to_all x1, blocking collectives, on_device(): lax.all_to_all(shaped.astype(jnp.bfloat16), 'row', split_axis=0, concat_a...  35.9 us
    all_to_all x1, blocking collectives, on_device(): lax.all_to_all(rounded, 'col', split_axis=1, concat_axis=0, tiled=True)  10.3 us
    dot_general x1, matrix products, on_device(): jnp.dot(regrouped, lax.all_gather(kept, 'col', axis=1, tiled=True), prefe...  3.53 us
  transfers between devices with their start and end apart: 1, of which 1 were waited for; matrix products, arithmetic and copies ran while one was open for 3% of the time, Pallas kernels for 0%

profile of v1, /device:TPU:1, one launch (start us, length us, event | category | flops | bytes accessed | tf_op | source)
XLA Modules:
  0.0 174.6 jit_solution(14745008950145160912)
XLA Ops:
  6.5 0.0 copy-start
  6.5 0.0 copy-start.1
  6.5 0.0 all-gather.2.cloned.1.call-start
  6.5 0.8 multiply_reduce_fusion
  7.4 0.1 convert_reduce_fusion
  7.5 0.1 broadcast_xor_fusion
  7.6 0.7 xor.32
  8.3 0.1 dynamic_slice.7
  8.4 0.1 dynamic_slice.6
  8.5 2.8 %compare_select_fusion.1 = bf16[2500,128]{1,0:T(8,128)(2,1)} fusion(bf16[2500,128]{1,0:T(8,128)(2,1)} %param.5, s32[128]{0:T(128)S(1)} %dynamic_slice.7, s32[2500]{0:T(1024)S(1)} %dynamic_slice.6), kind=kLoop, calls=%fused_computation.3 | loop fusion | flops 640000 | bytes 1290512 | tf_op jit(solution)/shard_map/jit(_where)/select_n | solution.py:35
  11.3 0.0 all-gather.2.cloned.1.call-update
  11.4 0.0 copy-done
  11.4 0.6 gather_fusion
  12.0 0.6 gather_fusion.1
  12.7 0.0 copy-done.1
  12.7 3.0 %compare_select_fusion = bf16[2,160000]{1,0:T(2,128)(2,1)S(1)} fusion(bf16[2,160000]{1,0:T(2,128)(2,1)S(1)} %copy-done.1, s32[160000]{0:T(1024)S(1)} %xor.32, s32[2]{0:T(128)S(1)} %xor.28), kind=kLoop, calls=%fused_computation.2 | loop fusion | flops 640000 | bytes 1920008 | tf_op jit(solution)/shard_map/jit(_where)/select_n | solution.py:29
  15.7 1.6 all_to_all.29
  17.4 0.7 copy.10
  18.1 53.9 %all_to_all.40 = bf16[2,64,2500]{2,0,1:T(2,128)(2,1)S(1)} all-to-all(bf16[2,64,2500]{2,0,1:T(2,128)(2,1)S(1)} %copy.10), channel_id=1, replica_groups=mesh['row'=64,'col'=8] {'row'}, dimensions={1} | all-to-all | bytes 1280000 | tf_op jit(solution)/shard_map/all_to_all | solution.py:32
  72.0 0.5 all_to_all.32
  72.5 44.8 %all-gather.2.cloned.1.call-done = bf16[2500,1024]{1,0:T(8,128)(2,1)} async-done(((bf16[2500,128]{1,0:T(8,128)(2,1)}), bf16[2500,1024]{1,0:T(8,128)(2,1)}) %all-gather.2.cloned.1.call-update) | async-done | bytes 5120016 | tf_op jit(solution)/shard_map/all_gather | solution.py:40
  117.3 3.5 %convolution_convert_fusion = bf16[128,1024]{1,0:T(8,128)(2,1)S(1)} fusion(bf16[128,2500]{1,0:T(8,128)(2,1)S(1)} %all_to_all.32, bf16[2500,1024]{1,0:T(8,128)(2,1)} %all-gather.2.cloned.1.call-done), kind=kOutput, calls=%fused_computation.4 | convolution fusion | flops 655491072 | bytes 6022144 | tf_op jit(solution)/shard_map/dot_general | solution.py:38
  120.8 0.1 convert_element_type.17
  120.9 35.9 %all_to_all.41 = bf16[64,16,128]{2,1,0:T(8,128)(2,1)S(1)} all-to-all(bf16[64,16,128]{2,1,0:T(8,128)(2,1)S(1)} %convert_element_type.17), channel_id=1, replica_groups=mesh['row'=64,'col'=8] {'row'}, dimensions={0} | all-to-all | bytes 524288 | tf_op jit(solution)/shard_map/all_to_all | solution.py:44
  156.8 0.1 reduce_sum.32
  156.9 10.3 %all_to_all.42 = bf16[2,8,128]{2,0,1:T(2,128)(2,1)S(1)} all-to-all(bf16[2,8,128]{2,0,1:T(2,128)(2,1)S(1)} %copy.11), channel_id=1, replica_groups=mesh['row'=64,'col'=8] {'col'}, dimensions={1} | all-to-all | bytes 8192 | tf_op jit(solution)/shard_map/all_to_all | solution.py:49
  167.2 0.6 copy.13
  (5 shorter events, 0.0 us)
Async XLA Ops:
  6.5 4.9 %copy-start = (s32[50]{0:T(128)S(1)}, s32[50]{0:T(128)}, u32[]{:S(2)}) copy-start(s32[50]{0:T(128)} %param.6) | copy-start | bytes 604
  6.5 6.2 %copy-start.1 = (bf16[2,160000]{1,0:T(2,128)(2,1)S(1)}, bf16[2,160000]{1,0:T(2,128)(2,1)}, u32[]{:S(2)}) copy-start(bf16[2,160000]{1,0:T(2,128)(2,1)} %param.4) | copy-start | bytes 1920004
  6.5 110.7 %all-gather.2.cloned.1.call-start = ((), (), s32[]{:S(2)}) async-start(), calls=%async_computation.3 | async-start | bytes 5769216 | tf_op jit(solution)/shard_map/all_gather | solution.py:40
Sparse Core Ops, SparseCore 0:
  11.5 105.7 all-gather.1

commit v2 on v0

v2 whole, which is shorter than its diff:
```python
import jax
import jax.numpy as jnp
from jax import lax
from jax.experimental import pallas as pl
from jax.experimental.pallas import tpu as pltpu
from jax.sharding import Mesh, PartitionSpec as P

OCCUPIED = 50
VIRTUAL = 400
WIDTH = 160
RANGE = 2500
SEGMENTS = 7
WINDOWS = 13
MAIN = 128
REST = WIDTH - MAIN
TILES = 2 * WINDOWS
GROUPS = -(-TILES // 4)
DEPTH = (TILES + GROUPS) * MAIN
PAD = 304
SPAN = 416
BF16 = jnp.bfloat16
F32 = jnp.float32


def block_starts(size_ref):
    starts = [0]
    for k in range(3):
        starts.append(starts[-1] + size_ref[k])
    return starts


def block_of(starts, value):
    label = jnp.where(value >= starts[1], 1, 0)
    label = label + jnp.where(value >= starts[2], 1, 0)
    return label + jnp.where(value >= starts[3], 1, 0)


def column_label(starts, first):
    s = first + lax.broadcasted_iota(jnp.int32, (1, 128), 1)
    a = jnp.where(s >= VIRTUAL, 1, 0) + jnp.where(s >= 2 * VIRTUAL, 1, 0)
    return jnp.bitwise_xor(block_of(starts, a), block_of(starts, s - VIRTUAL * a))


def pack_integrals(place_ref, size_ref, b_ref, out_ref, pad_ref, pick_ref):
    xl, z, co, xh, y = [place_ref[i] for i in range(5)]
    starts = block_starts(size_ref)
    first = RANGE * (xl * 32 + z * 2 + co)
    orbital = first // VIRTUAL
    offset = first - orbital * VIRTUAL
    label = column_label(starts, (xh * 4 + y) * 128)
    whole = RANGE // 16 * 16
    pad_ref[0:PAD] = jnp.zeros((PAD, 128), BF16)
    pad_ref[PAD : PAD + whole] = b_ref[0:whole]
    tail = jnp.concatenate(
        [b_ref[whole:RANGE].astype(F32), jnp.zeros((whole + 16 - RANGE, 128), F32)], axis=0
    )
    pad_ref[PAD + whole : PAD + whole + 16] = tail.astype(BF16)
    rest = pad_ref.shape[0] - (PAD + whole + 16)
    pad_ref[PAD + whole + 16 :] = jnp.zeros((rest, 128), BF16)
    start = (PAD - offset) // 16 * 16
    shift = PAD - offset - start
    t = lax.broadcasted_iota(jnp.int32, (WIDTH, SPAN), 0)
    row = lax.broadcasted_iota(jnp.int32, (WIDTH, SPAN), 1)
    for k in range(4):
        hit = (row == t + (starts[k] + shift)) & (t < size_ref[k])
        pick_ref[k * WIDTH : (k + 1) * WIDTH] = jnp.where(hit, 1.0, 0.0).astype(BF16)
    for j in range(SEGMENTS):
        rows = pad_ref[pl.ds(pl.multiple_of(start + VIRTUAL * j, 16), SPAN), :]
        picked = jnp.dot(pick_ref[...], rows, preferred_element_type=F32)
        want = jnp.bitwise_xor(block_of(starts, orbital + j), label)
        kept = jnp.zeros((WIDTH, 128), F32)
        for k in range(4):
            kept = jnp.where(want == k, picked[k * WIDTH : (k + 1) * WIDTH], kept)
        out_ref[j] = kept.astype(BF16)


def pack_amplitudes(place_ref, size_ref, occ_ref, a_ref, out_ref, pick_ref, main_ref, rest_ref):
    xl, z, co, xh, y = [place_ref[i] for i in range(5)]
    starts = block_starts(size_ref)
    first = (xl * 32 + z * 2 + co) * 16 + (xh * 4 + y) * 2
    d = lax.broadcasted_iota(jnp.int32, (VIRTUAL, 2 * MAIN), 0)
    lane = lax.broadcasted_iota(jnp.int32, (VIRTUAL, 2 * MAIN), 1)
    t = jnp.where(lane < MAIN, lane, MAIN + lane % REST)
    for k in range(4):
        pick_ref[:, 2 * MAIN * k : 2 * MAIN * (k + 1)] = jnp.where(
            d == t + starts[k], 1.0, 0.0
        ).astype(BF16)
    orbital = block_of(starts, lax.broadcasted_iota(jnp.int32, (VIRTUAL, 1), 0))
    group = lax.broadcasted_iota(jnp.int32, (16, MAIN), 1) // REST
    for i in range(2):
        pair = first + i
        label = jnp.bitwise_xor(occ_ref[pair // OCCUPIED], occ_ref[pair % OCCUPIED])
        want = jnp.bitwise_xor(orbital, label)
        picked = jnp.dot(
            a_ref[i * VIRTUAL : (i + 1) * VIRTUAL], pick_ref[...], preferred_element_type=F32
        )
        kept = jnp.zeros((VIRTUAL, 2 * MAIN), F32)
        for k in range(4):
            kept = jnp.where(want == k, picked[:, 2 * MAIN * k : 2 * MAIN * (k + 1)], kept)
        main_ref[...] = kept[:, :MAIN]
        rest_ref[...] = kept[:, MAIN:]
        for v in range(GROUPS):
            packed = jnp.zeros((16, MAIN), F32)
            for m in range(4):
                w = 4 * v + m
                if w >= TILES:
                    continue
                c = w // WINDOWS * 200 + w % WINDOWS
                mains = [main_ref[pl.ds(c + 12 * h, 8, stride=25)] for h in range(2)]
                rests = [rest_ref[pl.ds(c + 12 * h, 8, stride=25)] for h in range(2)]
                out_ref[i, :, MAIN * w : MAIN * (w + 1)] = jnp.concatenate(mains, 0).astype(BF16)
                packed = jnp.where(group == m, jnp.concatenate(rests, 0), packed)
            lo = MAIN * (TILES + v)
            out_ref[i, :, lo : lo + MAIN] = packed.astype(BF16)


def multiply(place_ref, size_ref, label_ref, a_ref, own_ref, other_ref, out_ref, b_ref, sum_ref):
    xl, z, co, xh, y = [place_ref[i] for i in range(5)]
    starts = block_starts(size_ref)
    low = TILES * MAIN
    spare = DEPTH - low - TILES * REST
    b_ref[low + TILES * REST :] = jnp.zeros((spare, 256), BF16)
    for w in (0, 6, 12, 13, 19, 25):
        b_ref[w * MAIN : (w + 1) * MAIN] = jnp.zeros((MAIN, 256), BF16)
        b_ref[low + w * REST : low + (w + 1) * REST] = jnp.zeros((REST, 256), BF16)
    for flip_co, from_ref in ((0, own_ref), (1, other_ref)):
        for flip_xl in range(2):
            base = jnp.bitwise_xor(xl, flip_xl) * WINDOWS + jnp.bitwise_xor(co, flip_co) * 6
            for flip_xh in range(2):
                lanes = slice(flip_xh * 128, (flip_xh + 1) * 128)
                for j in range(SEGMENTS):
                    upper = pl.ds(pl.multiple_of((base + j) * MAIN, MAIN), MAIN)
                    lower = pl.ds(pl.multiple_of(low + (base + j) * REST, REST), REST)
                    head = from_ref[flip_xl, flip_xh, j, 0:MAIN]
                    tail = from_ref[flip_xl, flip_xh, j, MAIN:WIDTH]
                    if j in (0, 6):
                        head = head + b_ref[upper, lanes]
                        tail = tail + b_ref[lower, lanes]
                    b_ref[upper, lanes] = head
                    b_ref[lower, lanes] = tail
    total = jnp.dot(a_ref[...], b_ref[...], preferred_element_type=F32)
    for flip_xh in range(2):
        there = jnp.bitwise_xor(xh, flip_xh)
        label = column_label(starts, (there * 4 + y) * 128)
        part = jnp.where(
            label_ref[...] == label, total[:, flip_xh * 128 : (flip_xh + 1) * 128], 0.0
        )
        sum_ref[...] = part
        for yy in range(4):
            for zz in range(16):
                out_ref[zz, there, 2 * yy : 2 * yy + 2] = sum_ref[
                    32 * yy + 2 * zz : 32 * yy + 2 * zz + 2
                ]


def in_vmem(count):
    return [pl.BlockSpec(memory_space=pltpu.VMEM)] * count


def in_smem(count):
    return [pl.BlockSpec(memory_space=pltpu.SMEM)] * count


def call(kernel, out_shape, out_type, specs, scratch):
    return pl.pallas_call(
        kernel,
        out_shape=jax.ShapeDtypeStruct(out_shape, out_type),
        in_specs=specs,
        out_specs=pl.BlockSpec(memory_space=pltpu.VMEM),
        scratch_shapes=scratch,
        compiler_params=pltpu.CompilerParams(vmem_limit_bytes=40 * 1024 * 1024),
    )


def run_pack_integrals(place, block_sizes, integrals):
    return call(
        pack_integrals,
        (SEGMENTS, WIDTH, 128),
        BF16,
        in_smem(2) + in_vmem(1),
        [pltpu.VMEM((PAD + 6 * VIRTUAL + SPAN, 128), BF16), pltpu.VMEM((4 * WIDTH, SPAN), BF16)],
    )(place, block_sizes, integrals)


def run_pack_amplitudes(place, block_sizes, occ_irreps, amplitudes):
    return call(
        pack_amplitudes,
        (2, 16, DEPTH),
        BF16,
        in_smem(3) + in_vmem(1),
        [
            pltpu.VMEM((VIRTUAL, 8 * MAIN), BF16),
            pltpu.VMEM((VIRTUAL, MAIN), F32),
            pltpu.VMEM((VIRTUAL, MAIN), F32),
        ],
    )(place, block_sizes, occ_irreps, amplitudes.reshape(2 * VIRTUAL, VIRTUAL))


def run_multiply(place, block_sizes, labels, spread, own, other):
    return call(
        multiply,
        (16, 2, 8, 128),
        F32,
        in_smem(2) + in_vmem(4),
        [pltpu.VMEM((DEPTH, 256), BF16), pltpu.VMEM((128, 128), F32)],
    )(place, block_sizes, labels, spread, own, other)


def row_labels(place, occ_irreps):
    row = jnp.arange(128, dtype=jnp.int32)
    xl, z, co, xh, y = [place[i] for i in range(5)]
    pair = xl * 512 + (row // 2 % 16) * 32 + co * 16 + xh * 8 + (row // 32) * 2 + row % 2
    orbitals = jnp.arange(OCCUPIED, dtype=jnp.int32)[None, :]
    irreps = occ_irreps[None, :]
    one = jnp.sum(jnp.where((pair // OCCUPIED)[:, None] == orbitals, irreps, 0), axis=1)
    two = jnp.sum(jnp.where((pair % OCCUPIED)[:, None] == orbitals, irreps, 0), axis=1)
    return jnp.bitwise_xor(one, two)[:, None]


def swap(array, axis):
    return lax.ppermute(array, axis, [(0, 1), (1, 0)])


def on_device(amplitudes, integrals, occ_irreps, block_sizes):
    place = jnp.stack([lax.axis_index(n) for n in ("xl", "z", "co", "xh", "y")]).astype(jnp.int32)
    packed_b = run_pack_integrals(place, block_sizes, integrals)
    pair_b = jnp.stack([packed_b, swap(packed_b, "xh")])
    own_b = jnp.stack([pair_b, swap(pair_b, "xl")])
    other_b = swap(own_b, "co")
    packed_a = run_pack_amplitudes(place, block_sizes, occ_irreps, amplitudes)
    sent = packed_a.reshape(2, 2, 8, DEPTH).transpose(2, 1, 0, 3).reshape(16, 2, DEPTH)
    came = lax.all_to_all(sent, "z", split_axis=0, concat_axis=0, tiled=True)
    copies = jnp.broadcast_to(came.reshape(1, 32, DEPTH), (4, 32, DEPTH))
    spread = lax.all_to_all(copies, "y", split_axis=0, concat_axis=0, tiled=True)
    labels = row_labels(place, occ_irreps)
    parts = run_multiply(place, block_sizes, labels, spread.reshape(128, DEPTH), own_b, other_b)
    pieces = lax.all_to_all(
        parts.reshape(32, 8, 128), ("z", "xh"), split_axis=0, concat_axis=0, tiled=True
    )
    total = jnp.sum(pieces.reshape(16, 2, 8, 128), axis=0)
    return total.reshape(16, 128).astype(BF16)


def solution(mesh):
    split = Mesh(mesh.devices.reshape(2, 16, 2, 2, 4), ("xl", "z", "co", "xh", "y"))
    row, col = ("xl", "z", "co"), ("xh", "y")
    return jax.shard_map(
        on_device,
        mesh=split,
        in_specs=(P(row + col, None), P(row, col), P(), P()),
        out_specs=P(row, col),
        check_vma=False,
    )
```

time: 352 us -> 103 us (0.29)
  the two profiles are of different devices: /device:TPU:2 before, /device:TPU:8 now
where the time goes in v2:
time: 103 us
  waiting for transfers between devices  32.2 us (31%)
  starting transfers between devices  30.5 us (30%)
  blocking collectives  26.8 us (26%)
  local copies, waits for them, and re-layouts  6.38 us (6%)
  Pallas kernels  5.26 us (5%)
  other arithmetic  1.74 us (2%)
    all_to_all x1, blocking collectives, on_device(): lax.all_to_all(parts.reshape(32, 8, 128), ('z', 'xh'), split_axis=0, conc...  26.8 us
    all_to_all x1, waiting for transfers between devices, on_device(): came = lax.all_to_all(sent, 'z', split_axis=0, concat_axis=0, tiled=True)  15.8 us
    all_to_all x1, starting transfers between devices, on_device(): came = lax.all_to_all(sent, 'z', split_axis=0, concat_axis=0, tiled=True)  15.2 us
    ppermute x3, starting transfers between devices, swap(): return lax.ppermute(array, axis, [(0, 1), (1, 0)])  10.4 us
    all_to_all x1, waiting for transfers between devices, on_device(): lax.all_to_all(copies, 'y', split_axis=0, concat_axis=0, tiled=True)  9.37 us
    ppermute x3, waiting for transfers between devices, swap(): return lax.ppermute(array, axis, [(0, 1), (1, 0)])  7.04 us
    all_to_all x1, starting transfers between devices, on_device(): lax.all_to_all(copies, 'y', split_axis=0, concat_axis=0, tiled=True)  4.91 us
    reshape x1, local copies, waits for them, and re-layouts, run_pack_amplitudes(): amplitudes.reshape(2 * VIRTUAL, VIRTUAL)  2.36 us
  transfers between devices with their start and end apart: 5, of which 3 were waited for; matrix products, arithmetic and copies ran while one was open for 5% of the time, Pallas kernels for 2%

profile of v2, /device:TPU:8, one launch (start us, length us, event | category | flops | bytes accessed | tf_op | source)
XLA Modules:
  0.0 102.9 jit_solution(772350324246749686)
XLA Ops:
  0.0 0.1 stack.41.place_ref
  0.1 0.0 copy-start
  0.1 1.1 %copy-done = bf16[2500,128]{1,0:T(8,128)(2,1)S(1)} copy-done((bf16[2500,128]{1,0:T(8,128)(2,1)S(1)}, bf16[2500,128]{1,0:T(8,128)(2,1)}, u32[]{:S(2)}) %copy-start) | copy-done | bytes 640024
  1.2 0.0 copy-start.1
  1.2 0.7 copy-done.1
  1.8 0.0 copy-start.4
  1.8 2.0 %shard_map.47 = bf16[7,160,128]{2,1,0:T(8,128)(2,1)S(1)} custom-call(s32[5]{0:T(128)S(1)} %stack.41.place_ref, s32[4]{0:T(128)S(1)} %copy-done.1, bf16[2500,128]{1,0:T(8,128)(2,1)S(1)} %copy-done), custom_call_target="tpu_custom_call" | custom-call | tf_op jit(solution)/shard_map/pallas_call | solution.py:176
  3.9 4.9 %collective-permute-start = (bf16[7,160,128]{2,1,0:T(8,128)(2,1)S(1)}, bf16[7,160,128]{2,1,0:T(8,128)(2,1)S(1)}, u32[]{:S(2)}, u32[]{:S(2)}) collective-permute-start(bf16[7,160,128]{2,1,0:T(8,128)(2,1)S(1)} %shard_map.47), channel_id=1, source_target_pairs={{0,4},{4,0},{1,5},{5,1},{2,6},{6,2},{3,7},{7,3},{8,12},{12,8},{9,1... | collective-permute-start | bytes 860168 | tf_op jit(solution)/shard_map/ppermute | solution.py:221
  8.8 7.0 %collective-permute-done = bf16[7,160,128]{2,1,0:T(8,128)(2,1)S(1)} collective-permute-done((bf16[7,160,128]{2,1,0:T(8,128)(2,1)S(1)}, bf16[7,160,128]{2,1,0:T(8,128)(2,1)S(1)}, u32[]{:S(2)}, u32[]{:S(2)}) %collective-permute-start) | collective-permute-done | bytes 286752 | tf_op jit(solution)/shard_map/ppermute | solution.py:221
  15.8 0.9 fusion.8
  16.7 0.0 copy-start.2
  16.7 0.0 copy-start.3
  16.7 3.5 %collective-permute-start.1 = (bf16[2,7,160,128]{3,2,1,0:T(8,128)(2,1)}, bf16[2,7,160,128]{3,2,1,0:T(8,128)(2,1)S(1)}, u32[]{:S(2)}, u32[]{:S(2)}) collective-permute-start(bf16[2,7,160,128]{3,2,1,0:T(8,128)(2,1)} %get-tuple-element.8), channel_id=1, source_target_pairs={{0,256},{256,0},{1,257},{257,1},{2,258},{258,2},{3,259},{259,3},{4... | collective-permute-start | bytes 1720328 | tf_op jit(solution)/shard_map/ppermute | solution.py:221
  20.3 0.0 copy-done.4
  20.3 2.4 %reshape.95.a_ref = bf16[800,400]{1,0:T(8,128)(2,1)S(1)} reshape(bf16[2,160000]{1,0:T(2,128)(2,1)S(1)} %copy-done.4) | data formatting | bytes 1280000 | tf_op jit(solution)/shard_map/reshape | solution.py:196
  22.6 0.0 copy-done.2
  22.6 0.0 copy-done.3
  22.7 1.7 %shard_map.46 = bf16[2,16,4224]{2,1,0:T(8,128)(2,1)S(1)} custom-call(s32[5]{0:T(128)S(1)} %stack.41.place_ref, s32[4]{0:T(128)S(1)} %copy-done.2, s32[50]{0:T(128)S(1)} %copy-done.3, bf16[800,400]{1,0:T(8,128)(2,1)S(1)} %reshape.95.a_ref), custom_call_target="tpu_custom_call" | custom-call | tf_op jit(solution)/shard_map/pallas_call | solution.py:186
  24.3 0.9 copy.8
  25.2 15.2 %all-to-all-start = ((bf16[16,2,4224]{2,1,0:T(2,128)(2,1)}), bf16[16,2,4224]{2,1,0:T(2,128)(2,1)S(1)}, u32[]{:S(2)}, u32[]{:S(2)}) async-start(bf16[16,2,4224]{2,1,0:T(2,128)(2,1)} %bitcast.8), calls=%async_computation | async-start | bytes 540672 | tf_op jit(solution)/shard_map/all_to_all | solution.py:232
  40.4 0.0 collective-permute-done.1
  40.4 0.1 pad_maximum_fusion.own_ref
  40.6 1.9 %collective-permute-start.2 = (bf16[2,2,7,160,128]{4,3,2,1,0:T(8,128)(2,1)S(1)}, bf16[2,2,7,160,128]{4,3,2,1,0:T(8,128)(2,1)S(1)}, u32[]{:S(2)}, u32[]{:S(2)}) collective-permute-start(bf16[2,2,7,160,128]{4,3,2,1,0:T(8,128)(2,1)S(1)} %pad_maximum_fusion.own_ref), channel_id=1, source_target_pairs={{0,8},{8,0},{1,9},{9,1},{2,10},{10,2},{3,11},{11,3},{4,12},{12,4},... | collective-permute-start | bytes 3440648 | tf_op jit(solution)/shard_map/ppermute | solution.py:221
  42.5 15.8 %all-to-all-done = bf16[16,2,4224]{2,1,0:T(2,128)(2,1)S(1)} async-done(((bf16[16,2,4224]{2,1,0:T(2,128)(2,1)}), bf16[16,2,4224]{2,1,0:T(2,128)(2,1)S(1)}, u32[]{:S(2)}, u32[]{:S(2)}) %all-to-all-start) | async-done | bytes 270368 | tf_op jit(solution)/shard_map/all_to_all | solution.py:232
  58.3 0.1 broadcast_in_dim.30
  58.4 1.1 %broadcast_in_dim.31 = bf16[4,32,4224]{2,1,0:T(8,128)(2,1)} broadcast(bf16[32,4224]{1,0:T(8,128)(2,1)S(1)} %broadcast_in_dim.30), dimensions={1,2} | broadcast | bytes 1351680 | tf_op jit(solution)/shard_map/broadcast_in_dim | solution.py:233
  59.4 4.9 %all-to-all-start.1 = ((bf16[4,32,4224]{2,1,0:T(8,128)(2,1)}), bf16[4,32,4224]{2,1,0:T(8,128)(2,1)S(1)}, u32[]{:S(2)}, u32[]{:S(2)}) async-start(bf16[4,32,4224]{2,1,0:T(8,128)(2,1)} %broadcast_in_dim.31), calls=%async_computation.1 | async-start | bytes 2162688 | tf_op jit(solution)/shard_map/all_to_all | solution.py:234
  64.4 0.1 select_reduce_fusion
  64.5 0.1 copy.9.label_ref
  64.6 9.4 %all-to-all-done.1 = bf16[4,32,4224]{2,1,0:T(8,128)(2,1)S(1)} async-done(((bf16[4,32,4224]{2,1,0:T(8,128)(2,1)}), bf16[4,32,4224]{2,1,0:T(8,128)(2,1)S(1)}, u32[]{:S(2)}, u32[]{:S(2)}) %all-to-all-start.1) | async-done | bytes 1081376 | tf_op jit(solution)/shard_map/all_to_all | solution.py:234
  74.0 0.0 collective-permute-done.2.other_ref
  74.0 1.6 %shard_map.48 = f32[16,2,8,128]{3,2,1,0:T(8,128)S(1)} custom-call(s32[5]{0:T(128)S(1)} %stack.41.place_ref, s32[4]{0:T(128)S(1)} %copy-done.2, s32[128,1]{1,0:T(8,128)S(1)} %copy.9.label_ref, bf16[128,4224]{1,0:T(8,128)(2,1)S(1)} %bitcast.22, bf16[2,2,7,160,128]{4,3,2,1,0:T(8,128)(2,1)S(1)} %pad_maximum_fusion.own_ref, ...), custom_call_target="tpu_custom_call" | custom-call | tf_op jit(solution)/shard_map/pallas_call | solution.py:200
  75.6 26.8 %all_to_all.15 = f32[32,8,128]{2,1,0:T(8,128)S(1)} all-to-all(f32[32,8,128]{2,1,0:T(8,128)S(1)} %bitcast.25), channel_id=1, replica_groups=mesh['xl'=2,'z'=16,'co'=2,'xh'=2,'y'=4] {'z','xh'}, dimensions={0} | all-to-all | bytes 262144 | tf_op jit(solution)/shard_map/all_to_all | solution.py:237
  102.3 0.6 reduce_sum.29
  (2 shorter events, 0.0 us)
Async XLA Ops:
  0.1 1.1 %copy-start = (bf16[2500,128]{1,0:T(8,128)(2,1)S(1)}, bf16[2500,128]{1,0:T(8,128)(2,1)}, u32[]{:S(2)}) copy-start(bf16[2500,128]{1,0:T(8,128)(2,1)} %b_ref.1) | copy-start | bytes 1920004
  1.2 0.7 copy-start.1
  1.8 18.4 %copy-start.4 = (bf16[2,160000]{1,0:T(2,128)(2,1)S(1)}, bf16[2,160000]{1,0:T(2,128)(2,1)}, u32[]{:S(2)}) copy-start(bf16[2,160000]{1,0:T(2,128)(2,1)} %param.4) | copy-start | bytes 1920004
  3.9 12.0 %collective-permute-start = (bf16[7,160,128]{2,1,0:T(8,128)(2,1)S(1)}, bf16[7,160,128]{2,1,0:T(8,128)(2,1)S(1)}, u32[]{:S(2)}, u32[]{:S(2)}) collective-permute-start(bf16[7,160,128]{2,1,0:T(8,128)(2,1)S(1)} %shard_map.47), channel_id=1, source_target_pairs={{0,4},{4,0},{1,5},{5,1},{2,6},{6,2},{3,7},{7,3},{8,12},{12,8},{9,1... | collective-permute-start | bytes 860168 | tf_op jit(solution)/shard_map/ppermute | solution.py:221
  16.7 5.9 %copy-start.2 = (s32[4]{0:T(128)S(1)}, s32[4]{0:T(128)}, u32[]{:S(2)}) copy-start(s32[4]{0:T(128)} %size_ref.5) | copy-start | bytes 52
  16.7 5.9 %copy-start.3 = (s32[50]{0:T(128)S(1)}, s32[50]{0:T(128)}, u32[]{:S(2)}) copy-start(s32[50]{0:T(128)} %occ_ref.1) | copy-start | bytes 604
  16.7 23.7 %collective-permute-start.1 = (bf16[2,7,160,128]{3,2,1,0:T(8,128)(2,1)}, bf16[2,7,160,128]{3,2,1,0:T(8,128)(2,1)S(1)}, u32[]{:S(2)}, u32[]{:S(2)}) collective-permute-start(bf16[2,7,160,128]{3,2,1,0:T(8,128)(2,1)} %get-tuple-element.8), channel_id=1, source_target_pairs={{0,256},{256,0},{1,257},{257,1},{2,258},{258,2},{3,259},{259,3},{4... | collective-permute-start | bytes 1720328 | tf_op jit(solution)/shard_map/ppermute | solution.py:221
  25.2 33.0 %all-to-all-start = ((bf16[16,2,4224]{2,1,0:T(2,128)(2,1)}), bf16[16,2,4224]{2,1,0:T(2,128)(2,1)S(1)}, u32[]{:S(2)}, u32[]{:S(2)}) async-start(bf16[16,2,4224]{2,1,0:T(2,128)(2,1)} %bitcast.8), calls=%async_computation | async-start | bytes 540672 | tf_op jit(solution)/shard_map/all_to_all | solution.py:232
  40.6 33.4 %collective-permute-start.2 = (bf16[2,2,7,160,128]{4,3,2,1,0:T(8,128)(2,1)S(1)}, bf16[2,2,7,160,128]{4,3,2,1,0:T(8,128)(2,1)S(1)}, u32[]{:S(2)}, u32[]{:S(2)}) collective-permute-start(bf16[2,2,7,160,128]{4,3,2,1,0:T(8,128)(2,1)S(1)} %pad_maximum_fusion.own_ref), channel_id=1, source_target_pairs={{0,8},{8,0},{1,9},{9,1},{2,10},{10,2},{3,11},{11,3},{4,12},{12,4},... | collective-permute-start | bytes 3440648 | tf_op jit(solution)/shard_map/ppermute | solution.py:221
  59.4 14.5 %all-to-all-start.1 = ((bf16[4,32,4224]{2,1,0:T(8,128)(2,1)}), bf16[4,32,4224]{2,1,0:T(8,128)(2,1)S(1)}, u32[]{:S(2)}, u32[]{:S(2)}) async-start(bf16[4,32,4224]{2,1,0:T(8,128)(2,1)} %broadcast_in_dim.31), calls=%async_computation.1 | async-start | bytes 2162688 | tf_op jit(solution)/shard_map/all_to_all | solution.py:234

commit v3 on v2

--- a/solution.py
+++ b/solution.py
@@ -224,12 +224,17 @@
 def on_device(amplitudes, integrals, occ_irreps, block_sizes):
     place = jnp.stack([lax.axis_index(n) for n in ("xl", "z", "co", "xh", "y")]).astype(jnp.int32)
     packed_b = run_pack_integrals(place, block_sizes, integrals)
-    pair_b = jnp.stack([packed_b, swap(packed_b, "xh")])
-    own_b = jnp.stack([pair_b, swap(pair_b, "xl")])
-    other_b = swap(own_b, "co")
+    swapped_b = swap(packed_b, "xh")
+    amplitudes, packed_b = lax.optimization_barrier((amplitudes, packed_b))
     packed_a = run_pack_amplitudes(place, block_sizes, occ_irreps, amplitudes)
     sent = packed_a.reshape(2, 2, 8, DEPTH).transpose(2, 1, 0, 3).reshape(16, 2, DEPTH)
+    sent, packed_b = lax.optimization_barrier((sent, packed_b))
+    pair_b = jnp.stack([packed_b, swapped_b])
+    sent, pair_b = lax.optimization_barrier((sent, pair_b))
     came = lax.all_to_all(sent, "z", split_axis=0, concat_axis=0, tiled=True)
+    swapped_b = swap(pair_b, "xl")
+    own_b = jnp.stack([pair_b, swapped_b])
+    other_b = swap(own_b, "co")
     copies = jnp.broadcast_to(came.reshape(1, 32, DEPTH), (4, 32, DEPTH))
     spread = lax.all_to_all(copies, "y", split_axis=0, concat_axis=0, tiled=True)
     labels = row_labels(place, occ_irreps)

time: 103 us -> 97.4 us (0.946)
  waiting for transfers between devices: 32.2 us -> 27.2 us
    ppermute x3, waiting for transfers between devices: 7.04 us -> 2.05 us  [swap(): return lax.ppermute(array, axis, [(0, 1), (1, 0)])]
where the time goes in v3:
time: 97.4 us; the launch traced here: 97 us
  starting transfers between devices  30.4 us (31%)
  waiting for transfers between devices  27.2 us (28%)
  blocking collectives  26.8 us (28%)
  local copies, waits for them, and re-layouts  6.37 us (7%)
  Pallas kernels  5.27 us (5%)
    all_to_all x1, blocking collectives, on_device(): lax.all_to_all(parts.reshape(32, 8, 128), ('z', 'xh'), split_axis=0, conc...  26.8 us
    all_to_all x1, waiting for transfers between devices, on_device(): came = lax.all_to_all(sent, 'z', split_axis=0, concat_axis=0, tiled=True)  15.8 us
    all_to_all x1, starting transfers between devices, on_device(): came = lax.all_to_all(sent, 'z', split_axis=0, concat_axis=0, tiled=True)  15.2 us
    ppermute x3, starting transfers between devices, swap(): return lax.ppermute(array, axis, [(0, 1), (1, 0)])  10.3 us
    all_to_all x1, waiting for transfers between devices, on_device(): lax.all_to_all(copies, 'y', split_axis=0, concat_axis=0, tiled=True)  9.37 us
    all_to_all x1, starting transfers between devices, on_device(): lax.all_to_all(copies, 'y', split_axis=0, concat_axis=0, tiled=True)  4.91 us
    reshape x1, local copies, waits for them, and re-layouts, run_pack_amplitudes(): amplitudes.reshape(2 * VIRTUAL, VIRTUAL)  2.37 us
    ppermute x3, waiting for transfers between devices, swap(): return lax.ppermute(array, axis, [(0, 1), (1, 0)])  2.05 us
  transfers between devices with their start and end apart: 5, of which 3 were waited for; matrix products, arithmetic and copies ran while one was open for 5% of the time, Pallas kernels for 2%

profile of v3, /device:TPU:8, one launch (start us, length us, event | category | flops | bytes accessed | tf_op | source)
XLA Modules:
  0.0 97.0 jit_solution(9680619833361542109)
XLA Ops:
  0.0 0.1 stack.41.place_ref
  0.1 0.0 copy-start
  0.1 1.1 %copy-done = bf16[2500,128]{1,0:T(8,128)(2,1)S(1)} copy-done((bf16[2500,128]{1,0:T(8,128)(2,1)S(1)}, bf16[2500,128]{1,0:T(8,128)(2,1)}, u32[]{:S(2)}) %copy-start) | copy-done | bytes 640024
  1.2 0.0 copy-start.1
  1.2 0.7 copy-done.1
  1.8 0.0 copy-start.4
  1.8 0.0 copy-start.2
  1.8 0.0 copy-start.3
  1.8 2.0 %shard_map.46 = bf16[7,160,128]{2,1,0:T(8,128)(2,1)S(1)} custom-call(s32[5]{0:T(128)S(1)} %stack.41.place_ref, s32[4]{0:T(128)S(1)} %copy-done.1, bf16[2500,128]{1,0:T(8,128)(2,1)S(1)} %copy-done), custom_call_target="tpu_custom_call" | custom-call | tf_op jit(solution)/shard_map/pallas_call | solution.py:176
  3.9 4.9 %collective-permute-start = (bf16[7,160,128]{2,1,0:T(8,128)(2,1)S(1)}, bf16[7,160,128]{2,1,0:T(8,128)(2,1)S(1)}, u32[]{:S(2)}, u32[]{:S(2)}) collective-permute-start(bf16[7,160,128]{2,1,0:T(8,128)(2,1)S(1)} %shard_map.46), channel_id=1, source_target_pairs={{0,4},{4,0},{1,5},{5,1},{2,6},{6,2},{3,7},{7,3},{8,12},{12,8},{9,1... | collective-permute-start | bytes 860168 | tf_op jit(solution)/shard_map/ppermute | solution.py:221
  8.8 0.0 copy-done.4
  8.8 2.4 %reshape.95.a_ref = bf16[800,400]{1,0:T(8,128)(2,1)S(1)} reshape(bf16[2,160000]{1,0:T(2,128)(2,1)S(1)} %copy-done.4) | data formatting | bytes 1280000 | tf_op jit(solution)/shard_map/reshape | solution.py:196
  11.2 0.0 copy-done.2
  11.2 0.0 copy-done.3
  11.2 1.7 %shard_map.47 = bf16[2,16,4224]{2,1,0:T(8,128)(2,1)S(1)} custom-call(s32[5]{0:T(128)S(1)} %stack.41.place_ref, s32[4]{0:T(128)S(1)} %copy-done.2, s32[50]{0:T(128)S(1)} %copy-done.3, bf16[800,400]{1,0:T(8,128)(2,1)S(1)} %reshape.95.a_ref), custom_call_target="tpu_custom_call" | custom-call | tf_op jit(solution)/shard_map/pallas_call | solution.py:186
  12.9 0.9 copy.8
  13.8 2.0 %collective-permute-done = bf16[7,160,128]{2,1,0:T(8,128)(2,1)S(1)} collective-permute-done((bf16[7,160,128]{2,1,0:T(8,128)(2,1)S(1)}, bf16[7,160,128]{2,1,0:T(8,128)(2,1)S(1)}, u32[]{:S(2)}, u32[]{:S(2)}) %collective-permute-start) | collective-permute-done | bytes 286752 | tf_op jit(solution)/shard_map/ppermute | solution.py:221
  15.8 0.1 pad_maximum_fusion.1
  15.9 3.4 %collective-permute-start.1 = (bf16[2,7,160,128]{3,2,1,0:T(8,128)(2,1)S(1)}, bf16[2,7,160,128]{3,2,1,0:T(8,128)(2,1)S(1)}, u32[]{:S(2)}, u32[]{:S(2)}) collective-permute-start(bf16[2,7,160,128]{3,2,1,0:T(8,128)(2,1)S(1)} %pad_maximum_fusion.1), channel_id=1, source_target_pairs={{0,256},{256,0},{1,257},{257,1},{2,258},{258,2},{3,259},{259,3},{4... | collective-permute-start | bytes 1720328 | tf_op jit(solution)/shard_map/ppermute | solution.py:221
  19.3 15.2 %all-to-all-start = ((bf16[16,2,4224]{2,1,0:T(2,128)(2,1)}), bf16[16,2,4224]{2,1,0:T(2,128)(2,1)S(1)}, u32[]{:S(2)}, u32[]{:S(2)}) async-start(bf16[16,2,4224]{2,1,0:T(2,128)(2,1)} %bitcast.8), calls=%async_computation | async-start | bytes 540672 | tf_op jit(solution)/shard_map/all_to_all | solution.py:234
  34.5 0.0 collective-permute-done.1
  34.5 0.1 pad_maximum_fusion.own_ref
  34.6 1.9 %collective-permute-start.2 = (bf16[2,2,7,160,128]{4,3,2,1,0:T(8,128)(2,1)S(1)}, bf16[2,2,7,160,128]{4,3,2,1,0:T(8,128)(2,1)S(1)}, u32[]{:S(2)}, u32[]{:S(2)}) collective-permute-start(bf16[2,2,7,160,128]{4,3,2,1,0:T(8,128)(2,1)S(1)} %pad_maximum_fusion.own_ref), channel_id=1, source_target_pairs={{0,8},{8,0},{1,9},{9,1},{2,10},{10,2},{3,11},{11,3},{4,12},{12,4},... | collective-permute-start | bytes 3440648 | tf_op jit(solution)/shard_map/ppermute | solution.py:221
  36.6 15.8 %all-to-all-done = bf16[16,2,4224]{2,1,0:T(2,128)(2,1)S(1)} async-done(((bf16[16,2,4224]{2,1,0:T(2,128)(2,1)}), bf16[16,2,4224]{2,1,0:T(2,128)(2,1)S(1)}, u32[]{:S(2)}, u32[]{:S(2)}) %all-to-all-start) | async-done | bytes 270368 | tf_op jit(solution)/shard_map/all_to_all | solution.py:234
  52.4 0.1 broadcast_in_dim.30
  52.5 1.0 %broadcast_in_dim.31 = bf16[4,32,4224]{2,1,0:T(8,128)(2,1)} broadcast(bf16[32,4224]{1,0:T(8,128)(2,1)S(1)} %broadcast_in_dim.30), dimensions={1,2} | broadcast | bytes 1351680 | tf_op jit(solution)/shard_map/broadcast_in_dim | solution.py:238
  53.5 4.9 %all-to-all-start.1 = ((bf16[4,32,4224]{2,1,0:T(8,128)(2,1)}), bf16[4,32,4224]{2,1,0:T(8,128)(2,1)S(1)}, u32[]{:S(2)}, u32[]{:S(2)}) async-start(bf16[4,32,4224]{2,1,0:T(8,128)(2,1)} %broadcast_in_dim.31), calls=%async_computation.1 | async-start | bytes 2162688 | tf_op jit(solution)/shard_map/all_to_all | solution.py:239
  58.4 0.1 select_reduce_fusion
  58.5 0.1 copy.9.label_ref
  58.7 0.0 collective-permute-done.2.other_ref
  58.7 9.4 %all-to-all-done.1 = bf16[4,32,4224]{2,1,0:T(8,128)(2,1)S(1)} async-done(((bf16[4,32,4224]{2,1,0:T(8,128)(2,1)}), bf16[4,32,4224]{2,1,0:T(8,128)(2,1)S(1)}, u32[]{:S(2)}, u32[]{:S(2)}) %all-to-all-start.1) | async-done | bytes 1081376 | tf_op jit(solution)/shard_map/all_to_all | solution.py:239
  68.0 1.6 %shard_map.48 = f32[16,2,8,128]{3,2,1,0:T(8,128)S(1)} custom-call(s32[5]{0:T(128)S(1)} %stack.41.place_ref, s32[4]{0:T(128)S(1)} %copy-done.2, s32[128,1]{1,0:T(8,128)S(1)} %copy.9.label_ref, bf16[128,4224]{1,0:T(8,128)(2,1)S(1)} %bitcast.21, bf16[2,2,7,160,128]{4,3,2,1,0:T(8,128)(2,1)S(1)} %pad_maximum_fusion.own_ref, ...), custom_call_target="tpu_custom_call" | custom-call | tf_op jit(solution)/shard_map/pallas_call | solution.py:200
  69.6 26.8 %all_to_all.15 = f32[32,8,128]{2,1,0:T(8,128)S(1)} all-to-all(f32[32,8,128]{2,1,0:T(8,128)S(1)} %bitcast.24), channel_id=1, replica_groups=mesh['xl'=2,'z'=16,'co'=2,'xh'=2,'y'=4] {'z','xh'}, dimensions={0} | all-to-all | bytes 262144 | tf_op jit(solution)/shard_map/all_to_all | solution.py:242
  96.4 0.6 reduce_sum.29
  (2 shorter events, 0.0 us)
Async XLA Ops:
  0.1 1.1 %copy-start = (bf16[2500,128]{1,0:T(8,128)(2,1)S(1)}, bf16[2500,128]{1,0:T(8,128)(2,1)}, u32[]{:S(2)}) copy-start(bf16[2500,128]{1,0:T(8,128)(2,1)} %b_ref.1) | copy-start | bytes 1920004
  1.2 0.7 copy-start.1
  1.8 7.0 %copy-start.4 = (bf16[2,160000]{1,0:T(2,128)(2,1)S(1)}, bf16[2,160000]{1,0:T(2,128)(2,1)}, u32[]{:S(2)}) copy-start(bf16[2,160000]{1,0:T(2,128)(2,1)} %param.4) | copy-start | bytes 1920004
  1.8 9.4 %copy-start.2 = (s32[4]{0:T(128)S(1)}, s32[4]{0:T(128)}, u32[]{:S(2)}) copy-start(s32[4]{0:T(128)} %size_ref.5) | copy-start | bytes 52
  1.8 9.4 %copy-start.3 = (s32[50]{0:T(128)S(1)}, s32[50]{0:T(128)}, u32[]{:S(2)}) copy-start(s32[50]{0:T(128)} %occ_ref.1) | copy-start | bytes 604
  3.9 12.0 %collective-permute-start = (bf16[7,160,128]{2,1,0:T(8,128)(2,1)S(1)}, bf16[7,160,128]{2,1,0:T(8,128)(2,1)S(1)}, u32[]{:S(2)}, u32[]{:S(2)}) collective-permute-start(bf16[7,160,128]{2,1,0:T(8,128)(2,1)S(1)} %shard_map.46), channel_id=1, source_target_pairs={{0,4},{4,0},{1,5},{5,1},{2,6},{6,2},{3,7},{7,3},{8,12},{12,8},{9,1... | collective-permute-start | bytes 860168 | tf_op jit(solution)/shard_map/ppermute | solution.py:221
  15.9 18.6 %collective-permute-start.1 = (bf16[2,7,160,128]{3,2,1,0:T(8,128)(2,1)S(1)}, bf16[2,7,160,128]{3,2,1,0:T(8,128)(2,1)S(1)}, u32[]{:S(2)}, u32[]{:S(2)}) collective-permute-start(bf16[2,7,160,128]{3,2,1,0:T(8,128)(2,1)S(1)} %pad_maximum_fusion.1), channel_id=1, source_target_pairs={{0,256},{256,0},{1,257},{257,1},{2,258},{258,2},{3,259},{259,3},{4... | collective-permute-start | bytes 1720328 | tf_op jit(solution)/shard_map/ppermute | solution.py:221
  19.3 33.1 %all-to-all-start = ((bf16[16,2,4224]{2,1,0:T(2,128)(2,1)}), bf16[16,2,4224]{2,1,0:T(2,128)(2,1)S(1)}, u32[]{:S(2)}, u32[]{:S(2)}) async-start(bf16[16,2,4224]{2,1,0:T(2,128)(2,1)} %bitcast.8), calls=%async_computation | async-start | bytes 540672 | tf_op jit(solution)/shard_map/all_to_all | solution.py:234
  34.6 24.0 %collective-permute-start.2 = (bf16[2,2,7,160,128]{4,3,2,1,0:T(8,128)(2,1)S(1)}, bf16[2,2,7,160,128]{4,3,2,1,0:T(8,128)(2,1)S(1)}, u32[]{:S(2)}, u32[]{:S(2)}) collective-permute-start(bf16[2,2,7,160,128]{4,3,2,1,0:T(8,128)(2,1)S(1)} %pad_maximum_fusion.own_ref), channel_id=1, source_target_pairs={{0,8},{8,0},{1,9},{9,1},{2,10},{10,2},{3,11},{11,3},{4,12},{12,4},... | collective-permute-start | bytes 3440648 | tf_op jit(solution)/shard_map/ppermute | solution.py:221
  53.5 14.5 %all-to-all-start.1 = ((bf16[4,32,4224]{2,1,0:T(8,128)(2,1)}), bf16[4,32,4224]{2,1,0:T(8,128)(2,1)S(1)}, u32[]{:S(2)}, u32[]{:S(2)}) async-start(bf16[4,32,4224]{2,1,0:T(8,128)(2,1)} %broadcast_in_dim.31), calls=%async_computation.1 | async-start | bytes 2162688 | tf_op jit(solution)/shard_map/all_to_all | solution.py:239

commit v4 on v2

--- a/solution.py
+++ b/solution.py
@@ -114,7 +114,7 @@
             out_ref[i, :, lo : lo + MAIN] = packed.astype(BF16)
 
 
-def multiply(place_ref, size_ref, label_ref, a_ref, own_ref, other_ref, out_ref, b_ref, sum_ref):
+def multiply(place_ref, size_ref, label_ref, a_ref, b00_ref, b01_ref, b10_ref, b11_ref, out_ref, b_ref, sum_ref):
     xl, z, co, xh, y = [place_ref[i] for i in range(5)]
     starts = block_starts(size_ref)
     low = TILES * MAIN
@@ -123,16 +123,16 @@
     for w in (0, 6, 12, 13, 19, 25):
         b_ref[w * MAIN : (w + 1) * MAIN] = jnp.zeros((MAIN, 256), BF16)
         b_ref[low + w * REST : low + (w + 1) * REST] = jnp.zeros((REST, 256), BF16)
-    for flip_co, from_ref in ((0, own_ref), (1, other_ref)):
-        for flip_xl in range(2):
+    for flip_co, refs in ((0, (b00_ref, b10_ref)), (1, (b01_ref, b11_ref))):
+        for flip_xl, from_ref in enumerate(refs):
             base = jnp.bitwise_xor(xl, flip_xl) * WINDOWS + jnp.bitwise_xor(co, flip_co) * 6
             for flip_xh in range(2):
                 lanes = slice(flip_xh * 128, (flip_xh + 1) * 128)
                 for j in range(SEGMENTS):
                     upper = pl.ds(pl.multiple_of((base + j) * MAIN, MAIN), MAIN)
                     lower = pl.ds(pl.multiple_of(low + (base + j) * REST, REST), REST)
-                    head = from_ref[flip_xl, flip_xh, j, 0:MAIN]
-                    tail = from_ref[flip_xl, flip_xh, j, MAIN:WIDTH]
+                    head = from_ref[flip_xh, j, 0:MAIN]
+                    tail = from_ref[flip_xh, j, MAIN:WIDTH]
                     if j in (0, 6):
                         head = head + b_ref[upper, lanes]
                         tail = tail + b_ref[lower, lanes]
@@ -196,14 +196,14 @@
     )(place, block_sizes, occ_irreps, amplitudes.reshape(2 * VIRTUAL, VIRTUAL))
 
 
-def run_multiply(place, block_sizes, labels, spread, own, other):
+def run_multiply(place, block_sizes, labels, spread, blocks):
     return call(
         multiply,
         (16, 2, 8, 128),
         F32,
-        in_smem(2) + in_vmem(4),
+        in_smem(2) + in_vmem(6),
         [pltpu.VMEM((DEPTH, 256), BF16), pltpu.VMEM((128, 128), F32)],
-    )(place, block_sizes, labels, spread, own, other)
+    )(place, block_sizes, labels, spread, *blocks)
 
 
 def row_labels(place, occ_irreps):
@@ -223,17 +223,18 @@
 
 def on_device(amplitudes, integrals, occ_irreps, block_sizes):
     place = jnp.stack([lax.axis_index(n) for n in ("xl", "z", "co", "xh", "y")]).astype(jnp.int32)
+    packed_a = run_pack_amplitudes(place, block_sizes, occ_irreps, amplitudes)
+    sent = packed_a.reshape(2, 2, 8, DEPTH).transpose(2, 1, 0, 3).reshape(16, 2, DEPTH)
+    sent, integrals = lax.optimization_barrier((sent, integrals))
+    came = lax.all_to_all(sent, "z", split_axis=0, concat_axis=0, tiled=True)
     packed_b = run_pack_integrals(place, block_sizes, integrals)
     pair_b = jnp.stack([packed_b, swap(packed_b, "xh")])
-    own_b = jnp.stack([pair_b, swap(pair_b, "xl")])
-    other_b = swap(own_b, "co")
-    packed_a = run_pack_amplitudes(place, block_sizes, occ_irreps, amplitudes)
-    sent = packed_a.reshape(2, 2, 8, DEPTH).transpose(2, 1, 0, 3).reshape(16, 2, DEPTH)
-    came = lax.all_to_all(sent, "z", split_axis=0, concat_axis=0, tiled=True)
+    far_b = swap(pair_b, "xl")
     copies = jnp.broadcast_to(came.reshape(1, 32, DEPTH), (4, 32, DEPTH))
     spread = lax.all_to_all(copies, "y", split_axis=0, concat_axis=0, tiled=True)
+    blocks_b = [pair_b, swap(pair_b, "co"), far_b, swap(far_b, "co")]
     labels = row_labels(place, occ_irreps)
-    parts = run_multiply(place, block_sizes, labels, spread.reshape(128, DEPTH), own_b, other_b)
+    parts = run_multiply(place, block_sizes, labels, spread.reshape(128, DEPTH), blocks_b)
     pieces = lax.all_to_all(
         parts.reshape(32, 8, 128), ("z", "xh"), split_axis=0, concat_axis=0, tiled=True
     )

time: 103 us -> 89.5 us (0.87)
  waiting for transfers between devices: 32.2 us -> 15.2 us
  blocking collectives: 26.8 us -> 29.8 us
  starting transfers between devices: 30.5 us -> 32.3 us
    all_to_all x1, waiting for transfers between devices: 15.8 us -> 1.36 us  [on_device(): came = lax.all_to_all(sent, 'z', split_axis=0, concat_axis=0, tiled=True)]
    all_to_all x1, waiting for transfers between devices: 9.37 us -> 2.73 us  [on_device(): lax.all_to_all(copies, 'y', split_axis=0, concat_axis=0, tiled=True)]
    ppermute x3 -> x4, waiting for transfers between devices: 7.04 us -> 11.1 us  [swap(): return lax.ppermute(array, axis, [(0, 1), (1, 0)])]
    all_to_all x1, blocking collectives: 26.8 us -> 29.8 us  [on_device(): lax.all_to_all(parts.reshape(32, 8, 128), ('z', 'xh'), split_axis=0, conc...]
    ppermute x3 -> x4, starting transfers between devices: 10.4 us -> 12.1 us  [swap(): return lax.ppermute(array, axis, [(0, 1), (1, 0)])]
    unnamed x10 -> x6, local copies, waits for them, and re-layouts: 1.75 us -> 0.01 us
    reshape x1, local copies, waits for them, and re-layouts: 2.36 us -> 3.48 us  [run_pack_amplitudes(): amplitudes.reshape(2 * VIRTUAL, VIRTUAL)]
  transfers between devices with their start and end apart: 5 -> 6, of which waited for: 3 -> 5; matrix products, arithmetic and copies ran while one was open for 5% -> 2% of each run, Pallas kernels for 2% -> 2%
where the time goes in v4:
time: 89.5 us; the launch traced here: 89.1 us
  starting transfers between devices  32.3 us (36%)
  blocking collectives  29.8 us (33%)
  waiting for transfers between devices  15.2 us (17%)
  local copies, waits for them, and re-layouts  5.77 us (6%)
  Pallas kernels  5.21 us (6%)
    all_to_all x1, blocking collectives, on_device(): lax.all_to_all(parts.reshape(32, 8, 128), ('z', 'xh'), split_axis=0, conc...  29.8 us
    all_to_all x1, starting transfers between devices, on_device(): came = lax.all_to_all(sent, 'z', split_axis=0, concat_axis=0, tiled=True)  15.2 us
    ppermute x4, starting transfers between devices, swap(): return lax.ppermute(array, axis, [(0, 1), (1, 0)])  12.1 us
    ppermute x4, waiting for transfers between devices, swap(): return lax.ppermute(array, axis, [(0, 1), (1, 0)])  11.1 us
    all_to_all x1, starting transfers between devices, on_device(): lax.all_to_all(copies, 'y', split_axis=0, concat_axis=0, tiled=True)  4.91 us
    reshape x1, local copies, waits for them, and re-layouts, run_pack_amplitudes(): amplitudes.reshape(2 * VIRTUAL, VIRTUAL)  3.48 us
    all_to_all x1, waiting for transfers between devices, on_device(): lax.all_to_all(copies, 'y', split_axis=0, concat_axis=0, tiled=True)  2.73 us
    pallas_call x1, Pallas kernels, run_pack_integrals(): call(pack_integrals, (SEGMENTS, WIDTH, 128), BF16, in_smem(2) + in_vmem(1...  2.03 us
  transfers between devices with their start and end apart: 6, of which 5 were waited for; matrix products, arithmetic and copies ran while one was open for 2% of the time, Pallas kernels for 2%

profile of v4, /device:TPU:8, one launch (start us, length us, event | category | flops | bytes accessed | tf_op | source)
XLA Modules:
  0.0 89.1 jit_solution(15286215683626956192)
XLA Ops:
  0.0 0.0 copy-start.1
  0.0 0.0 copy-start.2
  0.0 3.5 %reshape.95.a_ref = bf16[800,400]{1,0:T(8,128)(2,1)S(1)} reshape(bf16[2,160000]{1,0:T(2,128)(2,1)} %param.4) | data formatting | bytes 1280000 | tf_op jit(solution)/shard_map/reshape | solution.py:196
  3.5 0.1 stack.32.place_ref
  3.6 0.0 copy-done.1
  3.6 0.0 copy-done.2
  3.6 0.0 copy-start
  3.6 1.6 %shard_map.46 = bf16[2,16,4224]{2,1,0:T(8,128)(2,1)S(1)} custom-call(s32[5]{0:T(128)S(1)} %stack.32.place_ref, s32[4]{0:T(128)S(1)} %copy-done.1, s32[50]{0:T(128)S(1)} %copy-done.2, bf16[800,400]{1,0:T(8,128)(2,1)S(1)} %reshape.95.a_ref), custom_call_target="tpu_custom_call" | custom-call | tf_op jit(solution)/shard_map/pallas_call | solution.py:186
  5.2 0.9 %copy.8 = bf16[2,2,8,4224]{3,0,1,2:T(2,128)(2,1)} copy(bf16[2,2,8,4224]{3,2,1,0:T(8,128)(2,1)S(1)} %bitcast.21) | data formatting | bytes 540672 | tf_op jit(solution)/shard_map/reshape | solution.py:227
  6.2 15.2 %all-to-all-start = ((bf16[16,2,4224]{2,1,0:T(2,128)(2,1)}), bf16[16,2,4224]{2,1,0:T(2,128)(2,1)S(1)}, u32[]{:S(2)}, u32[]{:S(2)}) async-start(bf16[16,2,4224]{2,1,0:T(2,128)(2,1)} %bitcast.8), calls=%async_computation | async-start | bytes 540672 | tf_op jit(solution)/shard_map/all_to_all | solution.py:229
  21.4 0.0 copy-done
  21.4 2.0 %shard_map.47 = bf16[7,160,128]{2,1,0:T(8,128)(2,1)S(1)} custom-call(s32[5]{0:T(128)S(1)} %stack.32.place_ref, s32[4]{0:T(128)S(1)} %copy-done.1, bf16[2500,128]{1,0:T(8,128)(2,1)S(1)} %copy-done), custom_call_target="tpu_custom_call" | custom-call | tf_op jit(solution)/shard_map/pallas_call | solution.py:176
  23.4 4.9 %collective-permute-start = (bf16[7,160,128]{2,1,0:T(8,128)(2,1)S(1)}, bf16[7,160,128]{2,1,0:T(8,128)(2,1)S(1)}, u32[]{:S(2)}, u32[]{:S(2)}) collective-permute-start(bf16[7,160,128]{2,1,0:T(8,128)(2,1)S(1)} %shard_map.47), channel_id=1, source_target_pairs={{0,4},{4,0},{1,5},{5,1},{2,6},{6,2},{3,7},{7,3},{8,12},{12,8},{9,1... | collective-permute-start | bytes 860168 | tf_op jit(solution)/shard_map/ppermute | solution.py:221
  28.3 6.8 %collective-permute-done = bf16[7,160,128]{2,1,0:T(8,128)(2,1)S(1)} collective-permute-done((bf16[7,160,128]{2,1,0:T(8,128)(2,1)S(1)}, bf16[7,160,128]{2,1,0:T(8,128)(2,1)S(1)}, u32[]{:S(2)}, u32[]{:S(2)}) %collective-permute-start) | collective-permute-done | bytes 286752 | tf_op jit(solution)/shard_map/ppermute | solution.py:221
  35.1 0.1 pad_maximum_fusion.b00_ref
  35.1 3.4 %collective-permute-start.2 = (bf16[2,7,160,128]{3,2,1,0:T(8,128)(2,1)S(1)}, bf16[2,7,160,128]{3,2,1,0:T(8,128)(2,1)S(1)}, u32[]{:S(2)}, u32[]{:S(2)}) collective-permute-start(bf16[2,7,160,128]{3,2,1,0:T(8,128)(2,1)S(1)} %pad_maximum_fusion.b00_ref), channel_id=1, source_target_pairs={{0,256},{256,0},{1,257},{257,1},{2,258},{258,2},{3,259},{259,3},{4... | collective-permute-start | bytes 1720328 | tf_op jit(solution)/shard_map/ppermute | solution.py:221
  38.6 1.4 %all-to-all-done = bf16[16,2,4224]{2,1,0:T(2,128)(2,1)S(1)} async-done(((bf16[16,2,4224]{2,1,0:T(2,128)(2,1)}), bf16[16,2,4224]{2,1,0:T(2,128)(2,1)S(1)}, u32[]{:S(2)}, u32[]{:S(2)}) %all-to-all-start) | async-done | bytes 270368 | tf_op jit(solution)/shard_map/all_to_all | solution.py:229
  39.9 0.1 broadcast_in_dim.30
  40.0 1.1 %broadcast_in_dim.31 = bf16[4,32,4224]{2,1,0:T(8,128)(2,1)} broadcast(bf16[32,4224]{1,0:T(8,128)(2,1)S(1)} %broadcast_in_dim.30), dimensions={1,2} | broadcast | bytes 1351680 | tf_op jit(solution)/shard_map/broadcast_in_dim | solution.py:233
  41.1 4.9 %all-to-all-start.1 = ((bf16[4,32,4224]{2,1,0:T(8,128)(2,1)}), bf16[4,32,4224]{2,1,0:T(8,128)(2,1)S(1)}, u32[]{:S(2)}, u32[]{:S(2)}) async-start(bf16[4,32,4224]{2,1,0:T(8,128)(2,1)} %broadcast_in_dim.31), calls=%async_computation.1 | async-start | bytes 2162688 | tf_op jit(solution)/shard_map/all_to_all | solution.py:234
  46.0 1.9 %collective-permute-start.1 = (bf16[2,7,160,128]{3,2,1,0:T(8,128)(2,1)S(1)}, bf16[2,7,160,128]{3,2,1,0:T(8,128)(2,1)S(1)}, u32[]{:S(2)}, u32[]{:S(2)}) collective-permute-start(bf16[2,7,160,128]{3,2,1,0:T(8,128)(2,1)S(1)} %pad_maximum_fusion.b00_ref), channel_id=1, source_target_pairs={{0,8},{8,0},{1,9},{9,1},{2,10},{10,2},{3,11},{11,3},{4,12},{12,4},... | collective-permute-start | bytes 1720328 | tf_op jit(solution)/shard_map/ppermute | solution.py:221
  47.9 2.7 %collective-permute-done.2.b10_ref = bf16[2,7,160,128]{3,2,1,0:T(8,128)(2,1)S(1)} collective-permute-done((bf16[2,7,160,128]{3,2,1,0:T(8,128)(2,1)S(1)}, bf16[2,7,160,128]{3,2,1,0:T(8,128)(2,1)S(1)}, u32[]{:S(2)}, u32[]{:S(2)}) %collective-permute-start.2) | collective-permute-done | bytes 573472 | tf_op jit(solution)/shard_map/ppermute | solution.py:221
  50.6 1.9 %collective-permute-start.3 = (bf16[2,7,160,128]{3,2,1,0:T(8,128)(2,1)S(1)}, bf16[2,7,160,128]{3,2,1,0:T(8,128)(2,1)S(1)}, u32[]{:S(2)}, u32[]{:S(2)}) collective-permute-start(bf16[2,7,160,128]{3,2,1,0:T(8,128)(2,1)S(1)} %collective-permute-done.2.b10_ref), channel_id=1, source_target_pairs={{0,8},{8,0},{1,9},{9,1},{2,10},{10,2},{3,11},{11,3},{4,12},{12,4},... | collective-permute-start | bytes 1720328 | tf_op jit(solution)/shard_map/ppermute | solution.py:221
  52.5 0.1 select_reduce_fusion
  52.6 0.1 copy.9.label_ref
  52.7 0.0 collective-permute-done.1.b01_ref
  52.7 1.7 %collective-permute-done.3.b11_ref = bf16[2,7,160,128]{3,2,1,0:T(8,128)(2,1)S(1)} collective-permute-done((bf16[2,7,160,128]{3,2,1,0:T(8,128)(2,1)S(1)}, bf16[2,7,160,128]{3,2,1,0:T(8,128)(2,1)S(1)}, u32[]{:S(2)}, u32[]{:S(2)}) %collective-permute-start.3) | collective-permute-done | bytes 573472 | tf_op jit(solution)/shard_map/ppermute | solution.py:221
  54.4 2.7 %all-to-all-done.1 = bf16[4,32,4224]{2,1,0:T(8,128)(2,1)S(1)} async-done(((bf16[4,32,4224]{2,1,0:T(8,128)(2,1)}), bf16[4,32,4224]{2,1,0:T(8,128)(2,1)S(1)}, u32[]{:S(2)}, u32[]{:S(2)}) %all-to-all-start.1) | async-done | bytes 1081376 | tf_op jit(solution)/shard_map/all_to_all | solution.py:234
  57.2 1.5 %shard_map.48 = f32[16,2,8,128]{3,2,1,0:T(8,128)S(1)} custom-call(s32[5]{0:T(128)S(1)} %stack.32.place_ref, s32[4]{0:T(128)S(1)} %copy-done.1, s32[128,1]{1,0:T(8,128)S(1)} %copy.9.label_ref, bf16[128,4224]{1,0:T(8,128)(2,1)S(1)} %bitcast.19, bf16[2,7,160,128]{3,2,1,0:T(8,128)(2,1)S(1)} %pad_maximum_fusion.b00_ref, ...), custom_call_target="tpu_custom_call" | custom-call | tf_op jit(solution)/shard_map/pallas_call | solution.py:200
  58.7 29.8 %all_to_all.15 = f32[32,8,128]{2,1,0:T(8,128)S(1)} all-to-all(f32[32,8,128]{2,1,0:T(8,128)S(1)} %bitcast.22), channel_id=1, replica_groups=mesh['xl'=2,'z'=16,'co'=2,'xh'=2,'y'=4] {'z','xh'}, dimensions={0} | all-to-all | bytes 262144 | tf_op jit(solution)/shard_map/all_to_all | solution.py:238
  88.5 0.6 reduce_sum.29
  (2 shorter events, 0.0 us)
Async XLA Ops:
  0.0 3.6 %copy-start.1 = (s32[4]{0:T(128)S(1)}, s32[4]{0:T(128)}, u32[]{:S(2)}) copy-start(s32[4]{0:T(128)} %size_ref.5) | copy-start | bytes 52
  0.0 3.6 %copy-start.2 = (s32[50]{0:T(128)S(1)}, s32[50]{0:T(128)}, u32[]{:S(2)}) copy-start(s32[50]{0:T(128)} %occ_ref.1) | copy-start | bytes 604
  3.6 17.8 %copy-start = (bf16[2500,128]{1,0:T(8,128)(2,1)S(1)}, bf16[2500,128]{1,0:T(8,128)(2,1)}, u32[]{:S(2)}) copy-start(bf16[2500,128]{1,0:T(8,128)(2,1)} %b_ref) | copy-start | bytes 1920004
  6.2 33.8 %all-to-all-start = ((bf16[16,2,4224]{2,1,0:T(2,128)(2,1)}), bf16[16,2,4224]{2,1,0:T(2,128)(2,1)S(1)}, u32[]{:S(2)}, u32[]{:S(2)}) async-start(bf16[16,2,4224]{2,1,0:T(2,128)(2,1)} %bitcast.8), calls=%async_computation | async-start | bytes 540672 | tf_op jit(solution)/shard_map/all_to_all | solution.py:229
  23.4 11.7 %collective-permute-start = (bf16[7,160,128]{2,1,0:T(8,128)(2,1)S(1)}, bf16[7,160,128]{2,1,0:T(8,128)(2,1)S(1)}, u32[]{:S(2)}, u32[]{:S(2)}) collective-permute-start(bf16[7,160,128]{2,1,0:T(8,128)(2,1)S(1)} %shard_map.47), channel_id=1, source_target_pairs={{0,4},{4,0},{1,5},{5,1},{2,6},{6,2},{3,7},{7,3},{8,12},{12,8},{9,1... | collective-permute-start | bytes 860168 | tf_op jit(solution)/shard_map/ppermute | solution.py:221
  35.1 15.4 %collective-permute-start.2 = (bf16[2,7,160,128]{3,2,1,0:T(8,128)(2,1)S(1)}, bf16[2,7,160,128]{3,2,1,0:T(8,128)(2,1)S(1)}, u32[]{:S(2)}, u32[]{:S(2)}) collective-permute-start(bf16[2,7,160,128]{3,2,1,0:T(8,128)(2,1)S(1)} %pad_maximum_fusion.b00_ref), channel_id=1, source_target_pairs={{0,256},{256,0},{1,257},{257,1},{2,258},{258,2},{3,259},{259,3},{4... | collective-permute-start | bytes 1720328 | tf_op jit(solution)/shard_map/ppermute | solution.py:221
  41.1 16.1 %all-to-all-start.1 = ((bf16[4,32,4224]{2,1,0:T(8,128)(2,1)}), bf16[4,32,4224]{2,1,0:T(8,128)(2,1)S(1)}, u32[]{:S(2)}, u32[]{:S(2)}) async-start(bf16[4,32,4224]{2,1,0:T(8,128)(2,1)} %broadcast_in_dim.31), calls=%async_computation.1 | async-start | bytes 2162688 | tf_op jit(solution)/shard_map/all_to_all | solution.py:234
  46.0 6.8 %collective-permute-start.1 = (bf16[2,7,160,128]{3,2,1,0:T(8,128)(2,1)S(1)}, bf16[2,7,160,128]{3,2,1,0:T(8,128)(2,1)S(1)}, u32[]{:S(2)}, u32[]{:S(2)}) collective-permute-start(bf16[2,7,160,128]{3,2,1,0:T(8,128)(2,1)S(1)} %pad_maximum_fusion.b00_ref), channel_id=1, source_target_pairs={{0,8},{8,0},{1,9},{9,1},{2,10},{10,2},{3,11},{11,3},{4,12},{12,4},... | collective-permute-start | bytes 1720328 | tf_op jit(solution)/shard_map/ppermute | solution.py:221
  50.6 3.9 %collective-permute-start.3 = (bf16[2,7,160,128]{3,2,1,0:T(8,128)(2,1)S(1)}, bf16[2,7,160,128]{3,2,1,0:T(8,128)(2,1)S(1)}, u32[]{:S(2)}, u32[]{:S(2)}) collective-permute-start(bf16[2,7,160,128]{3,2,1,0:T(8,128)(2,1)S(1)} %collective-permute-done.2.b10_ref), channel_id=1, source_target_pairs={{0,8},{8,0},{1,9},{9,1},{2,10},{10,2},{3,11},{11,3},{4,12},{12,4},... | collective-permute-start | bytes 1720328 | tf_op jit(solution)/shard_map/ppermute | solution.py:221

commit v5 on v4

--- a/solution.py
+++ b/solution.py
@@ -17,7 +17,6 @@
 GROUPS = -(-TILES // 4)
 DEPTH = (TILES + GROUPS) * MAIN
 PAD = 304
-SPAN = 416
 BF16 = jnp.bfloat16
 F32 = jnp.float32
 
@@ -41,37 +40,27 @@
     return jnp.bitwise_xor(block_of(starts, a), block_of(starts, s - VIRTUAL * a))
 
 
-def pack_integrals(place_ref, size_ref, b_ref, out_ref, pad_ref, pick_ref):
+def pack_integrals(place_ref, size_ref, b_ref, out_ref, pad_ref):
     xl, z, co, xh, y = [place_ref[i] for i in range(5)]
     starts = block_starts(size_ref)
     first = RANGE * (xl * 32 + z * 2 + co)
     orbital = first // VIRTUAL
     offset = first - orbital * VIRTUAL
     label = column_label(starts, (xh * 4 + y) * 128)
-    whole = RANGE // 16 * 16
-    pad_ref[0:PAD] = jnp.zeros((PAD, 128), BF16)
-    pad_ref[PAD : PAD + whole] = b_ref[0:whole]
-    tail = jnp.concatenate(
-        [b_ref[whole:RANGE].astype(F32), jnp.zeros((whole + 16 - RANGE, 128), F32)], axis=0
-    )
-    pad_ref[PAD + whole : PAD + whole + 16] = tail.astype(BF16)
-    rest = pad_ref.shape[0] - (PAD + whole + 16)
-    pad_ref[PAD + whole + 16 :] = jnp.zeros((rest, 128), BF16)
-    start = (PAD - offset) // 16 * 16
-    shift = PAD - offset - start
-    t = lax.broadcasted_iota(jnp.int32, (WIDTH, SPAN), 0)
-    row = lax.broadcasted_iota(jnp.int32, (WIDTH, SPAN), 1)
-    for k in range(4):
-        hit = (row == t + (starts[k] + shift)) & (t < size_ref[k])
-        pick_ref[k * WIDTH : (k + 1) * WIDTH] = jnp.where(hit, 1.0, 0.0).astype(BF16)
+    after = pad_ref.shape[0] - PAD - RANGE
+    pad_ref[0:PAD] = jnp.zeros((PAD, 128), F32)
+    pad_ref[PAD + RANGE :] = jnp.zeros((after, 128), F32)
+    pad_ref[PAD : PAD + RANGE] = b_ref[...].astype(F32)
+    t = lax.broadcasted_iota(jnp.int32, (WIDTH, 128), 0)
     for j in range(SEGMENTS):
-        rows = pad_ref[pl.ds(pl.multiple_of(start + VIRTUAL * j, 16), SPAN), :]
-        picked = jnp.dot(pick_ref[...], rows, preferred_element_type=F32)
         want = jnp.bitwise_xor(block_of(starts, orbital + j), label)
         kept = jnp.zeros((WIDTH, 128), F32)
+        length = jnp.zeros((1, 128), jnp.int32)
         for k in range(4):
-            kept = jnp.where(want == k, picked[k * WIDTH : (k + 1) * WIDTH], kept)
-        out_ref[j] = kept.astype(BF16)
+            rows = pad_ref[pl.ds(PAD - offset + VIRTUAL * j + starts[k], WIDTH), :]
+            kept = jnp.where(want == k, rows, kept)
+            length = jnp.where(want == k, size_ref[k], length)
+        out_ref[j] = jnp.where(t < length, kept, 0.0).astype(BF16)
 
 
 def pack_amplitudes(place_ref, size_ref, occ_ref, a_ref, out_ref, pick_ref, main_ref, rest_ref):
@@ -106,8 +95,9 @@
                 if w >= TILES:
                     continue
                 c = w // WINDOWS * 200 + w % WINDOWS
-                mains = [main_ref[pl.ds(c + 12 * h, 8, stride=25)] for h in range(2)]
-                rests = [rest_ref[pl.ds(c + 12 * h, 8, stride=25)] for h in range(2)]
+                places = [pl.ds(c + 12 * h + 25 * u, 4, stride=25) for h in range(2) for u in (4, 0)]
+                mains = [main_ref[rows] for rows in places]
+                rests = [rest_ref[rows] for rows in places]
                 out_ref[i, :, MAIN * w : MAIN * (w + 1)] = jnp.concatenate(mains, 0).astype(BF16)
                 packed = jnp.where(group == m, jnp.concatenate(rests, 0), packed)
             lo = MAIN * (TILES + v)
@@ -148,7 +138,7 @@
         sum_ref[...] = part
         for yy in range(4):
             for zz in range(16):
-                out_ref[zz, there, 2 * yy : 2 * yy + 2] = sum_ref[
+                out_ref[(zz + 8) % 16, there, 2 * yy : 2 * yy + 2] = sum_ref[
                     32 * yy + 2 * zz : 32 * yy + 2 * zz + 2
                 ]
 
@@ -178,7 +168,7 @@
         (SEGMENTS, WIDTH, 128),
         BF16,
         in_smem(2) + in_vmem(1),
-        [pltpu.VMEM((PAD + 6 * VIRTUAL + SPAN, 128), BF16), pltpu.VMEM((4 * WIDTH, SPAN), BF16)],
+        [pltpu.VMEM((PAD + SEGMENTS * VIRTUAL + WIDTH, 128), F32)],
     )(place, block_sizes, integrals)
 
 
@@ -209,7 +199,7 @@
 def row_labels(place, occ_irreps):
     row = jnp.arange(128, dtype=jnp.int32)
     xl, z, co, xh, y = [place[i] for i in range(5)]
-    pair = xl * 512 + (row // 2 % 16) * 32 + co * 16 + xh * 8 + (row // 32) * 2 + row % 2
+    pair = xl * 512 + ((row // 2 + 8) % 16) * 32 + co * 16 + xh * 8 + (row // 32) * 2 + row % 2
     orbitals = jnp.arange(OCCUPIED, dtype=jnp.int32)[None, :]
     irreps = occ_irreps[None, :]
     one = jnp.sum(jnp.where((pair // OCCUPIED)[:, None] == orbitals, irreps, 0), axis=1)
@@ -226,7 +216,9 @@
     packed_a = run_pack_amplitudes(place, block_sizes, occ_irreps, amplitudes)
     sent = packed_a.reshape(2, 2, 8, DEPTH).transpose(2, 1, 0, 3).reshape(16, 2, DEPTH)
     sent, integrals = lax.optimization_barrier((sent, integrals))
-    came = lax.all_to_all(sent, "z", split_axis=0, concat_axis=0, tiled=True)
+    came = lax.all_to_all(
+        sent, "z", split_axis=0, concat_axis=0, tiled=True, axis_index_groups=[[(i + 8) % 16 for i in range(16)]]
+    )
     packed_b = run_pack_integrals(place, block_sizes, integrals)
     pair_b = jnp.stack([packed_b, swap(packed_b, "xh")])
     far_b = swap(pair_b, "xl")

time: 89.5 us -> 85.9 us (0.960)
  the two profiles are of different devices: /device:TPU:8 before, /device:TPU:2 now
where the time goes in v5:
time: 85.9 us; the launch traced here: 85.4 us
  starting transfers between devices  33.6 us (39%)
  blocking collectives  24.1 us (28%)
  waiting for transfers between devices  17 us (20%)
  local copies, waits for them, and re-layouts  5.77 us (7%)
  Pallas kernels  4.09 us (5%)
    all_to_all x1, blocking collectives, on_device(): lax.all_to_all(parts.reshape(32, 8, 128), ('z', 'xh'), split_axis=0, conc...  24.1 us
    all_to_all x1, starting transfers between devices, on_device(): lax.all_to_all(sent, 'z', split_axis=0, concat_axis=0, tiled=True, axis_i...  18.9 us
    ppermute x4, waiting for transfers between devices, swap(): return lax.ppermute(array, axis, [(0, 1), (1, 0)])  14.2 us
    ppermute x4, starting transfers between devices, swap(): return lax.ppermute(array, axis, [(0, 1), (1, 0)])  10.3 us
    all_to_all x1, starting transfers between devices, on_device(): lax.all_to_all(copies, 'y', split_axis=0, concat_axis=0, tiled=True)  4.46 us
    reshape x1, local copies, waits for them, and re-layouts, run_pack_amplitudes(): amplitudes.reshape(2 * VIRTUAL, VIRTUAL)  3.48 us
    all_to_all x1, waiting for transfers between devices, on_device(): lax.all_to_all(copies, 'y', split_axis=0, concat_axis=0, tiled=True)  2.78 us
    pallas_call x1, Pallas kernels, run_pack_amplitudes(): call(pack_amplitudes, (2, 16, DEPTH), BF16, in_smem(3) + in_vmem(1), [plt...  1.72 us
  transfers between devices with their start and end apart: 6, of which 4 were waited for; matrix products, arithmetic and copies ran while one was open for 2% of the time, Pallas kernels for 1%

profile of v5, /device:TPU:2, one launch (start us, length us, event | category | flops | bytes accessed | tf_op | source)
XLA Modules:
  0.0 85.4 jit_solution(11074552406324340969)
XLA Ops:
  0.0 0.0 copy-start.1
  0.0 0.0 copy-start.2
  0.0 3.5 %reshape.96.a_ref = bf16[800,400]{1,0:T(8,128)(2,1)S(1)} reshape(bf16[2,160000]{1,0:T(2,128)(2,1)} %param.4) | data formatting | bytes 1280000 | tf_op jit(solution)/shard_map/reshape | solution.py:186
  3.5 0.1 stack.32.place_ref
  3.6 0.0 copy-done.1
  3.6 0.0 copy-done.2
  3.6 0.0 copy-start
  3.6 1.7 %shard_map.46 = bf16[2,16,4224]{2,1,0:T(8,128)(2,1)S(1)} custom-call(s32[5]{0:T(128)S(1)} %stack.32.place_ref, s32[4]{0:T(128)S(1)} %copy-done.1, s32[50]{0:T(128)S(1)} %copy-done.2, bf16[800,400]{1,0:T(8,128)(2,1)S(1)} %reshape.96.a_ref), custom_call_target="tpu_custom_call" | custom-call | tf_op jit(solution)/shard_map/pallas_call | solution.py:176
  5.3 0.9 %copy.8 = bf16[2,2,8,4224]{3,0,1,2:T(2,128)(2,1)} copy(bf16[2,2,8,4224]{3,2,1,0:T(8,128)(2,1)S(1)} %bitcast.21) | data formatting | bytes 540672 | tf_op jit(solution)/shard_map/reshape | solution.py:217
  6.2 18.9 %all-to-all-start = ((bf16[16,2,4224]{2,1,0:T(2,128)(2,1)}), bf16[16,2,4224]{2,1,0:T(2,128)(2,1)S(1)}, u32[]{:S(2)}, u32[]{:S(2)}) async-start(bf16[16,2,4224]{2,1,0:T(2,128)(2,1)} %bitcast.8), calls=%async_computation | async-start | bytes 540672 | tf_op jit(solution)/shard_map/all_to_all | solution.py:219
  25.1 0.0 copy-done
  25.1 0.8 shard_map.47
  25.9 4.0 %collective-permute-start = (bf16[7,160,128]{2,1,0:T(8,128)(2,1)S(1)}, bf16[7,160,128]{2,1,0:T(8,128)(2,1)S(1)}, u32[]{:S(2)}, u32[]{:S(2)}) collective-permute-start(bf16[7,160,128]{2,1,0:T(8,128)(2,1)S(1)} %shard_map.47), channel_id=1, source_target_pairs={{0,4},{4,0},{1,5},{5,1},{2,6},{6,2},{3,7},{7,3},{8,12},{12,8},{9,1... | collective-permute-start | bytes 860168 | tf_op jit(solution)/shard_map/ppermute | solution.py:211
  30.0 7.4 %collective-permute-done = bf16[7,160,128]{2,1,0:T(8,128)(2,1)S(1)} collective-permute-done((bf16[7,160,128]{2,1,0:T(8,128)(2,1)S(1)}, bf16[7,160,128]{2,1,0:T(8,128)(2,1)S(1)}, u32[]{:S(2)}, u32[]{:S(2)}) %collective-permute-start) | collective-permute-done | bytes 286752 | tf_op jit(solution)/shard_map/ppermute | solution.py:211
  37.3 0.1 pad_maximum_fusion.b00_ref
  37.4 2.4 %collective-permute-start.2 = (bf16[2,7,160,128]{3,2,1,0:T(8,128)(2,1)S(1)}, bf16[2,7,160,128]{3,2,1,0:T(8,128)(2,1)S(1)}, u32[]{:S(2)}, u32[]{:S(2)}) collective-permute-start(bf16[2,7,160,128]{3,2,1,0:T(8,128)(2,1)S(1)} %pad_maximum_fusion.b00_ref), channel_id=1, source_target_pairs={{0,256},{256,0},{1,257},{257,1},{2,258},{258,2},{3,259},{259,3},{4... | collective-permute-start | bytes 1720328 | tf_op jit(solution)/shard_map/ppermute | solution.py:211
  39.8 0.0 all-to-all-done
  39.9 0.1 broadcast_in_dim.30
  40.0 1.1 %broadcast_in_dim.31 = bf16[4,32,4224]{2,1,0:T(8,128)(2,1)} broadcast(bf16[32,4224]{1,0:T(8,128)(2,1)S(1)} %broadcast_in_dim.30), dimensions={1,2} | broadcast | bytes 1351680 | tf_op jit(solution)/shard_map/broadcast_in_dim | solution.py:225
  41.0 4.5 %all-to-all-start.1 = ((bf16[4,32,4224]{2,1,0:T(8,128)(2,1)}), bf16[4,32,4224]{2,1,0:T(8,128)(2,1)S(1)}, u32[]{:S(2)}, u32[]{:S(2)}) async-start(bf16[4,32,4224]{2,1,0:T(8,128)(2,1)} %broadcast_in_dim.31), calls=%async_computation.1 | async-start | bytes 2162688 | tf_op jit(solution)/shard_map/all_to_all | solution.py:226
  45.5 1.9 %collective-permute-start.1 = (bf16[2,7,160,128]{3,2,1,0:T(8,128)(2,1)S(1)}, bf16[2,7,160,128]{3,2,1,0:T(8,128)(2,1)S(1)}, u32[]{:S(2)}, u32[]{:S(2)}) collective-permute-start(bf16[2,7,160,128]{3,2,1,0:T(8,128)(2,1)S(1)} %pad_maximum_fusion.b00_ref), channel_id=1, source_target_pairs={{0,8},{8,0},{1,9},{9,1},{2,10},{10,2},{3,11},{11,3},{4,12},{12,4},... | collective-permute-start | bytes 1720328 | tf_op jit(solution)/shard_map/ppermute | solution.py:211
  47.4 5.1 %collective-permute-done.2.b10_ref = bf16[2,7,160,128]{3,2,1,0:T(8,128)(2,1)S(1)} collective-permute-done((bf16[2,7,160,128]{3,2,1,0:T(8,128)(2,1)S(1)}, bf16[2,7,160,128]{3,2,1,0:T(8,128)(2,1)S(1)}, u32[]{:S(2)}, u32[]{:S(2)}) %collective-permute-start.2) | collective-permute-done | bytes 573472 | tf_op jit(solution)/shard_map/ppermute | solution.py:211
  52.5 1.9 %collective-permute-start.3 = (bf16[2,7,160,128]{3,2,1,0:T(8,128)(2,1)S(1)}, bf16[2,7,160,128]{3,2,1,0:T(8,128)(2,1)S(1)}, u32[]{:S(2)}, u32[]{:S(2)}) collective-permute-start(bf16[2,7,160,128]{3,2,1,0:T(8,128)(2,1)S(1)} %collective-permute-done.2.b10_ref), channel_id=1, source_target_pairs={{0,8},{8,0},{1,9},{9,1},{2,10},{10,2},{3,11},{11,3},{4,12},{12,4},... | collective-permute-start | bytes 1720328 | tf_op jit(solution)/shard_map/ppermute | solution.py:211
  54.5 0.1 select_reduce_fusion
  54.6 0.1 copy.9.label_ref
  54.7 0.0 collective-permute-done.1.b01_ref
  54.7 1.7 %collective-permute-done.3.b11_ref = bf16[2,7,160,128]{3,2,1,0:T(8,128)(2,1)S(1)} collective-permute-done((bf16[2,7,160,128]{3,2,1,0:T(8,128)(2,1)S(1)}, bf16[2,7,160,128]{3,2,1,0:T(8,128)(2,1)S(1)}, u32[]{:S(2)}, u32[]{:S(2)}) %collective-permute-start.3) | collective-permute-done | bytes 573472 | tf_op jit(solution)/shard_map/ppermute | solution.py:211
  56.4 2.8 %all-to-all-done.1 = bf16[4,32,4224]{2,1,0:T(8,128)(2,1)S(1)} async-done(((bf16[4,32,4224]{2,1,0:T(8,128)(2,1)}), bf16[4,32,4224]{2,1,0:T(8,128)(2,1)S(1)}, u32[]{:S(2)}, u32[]{:S(2)}) %all-to-all-start.1) | async-done | bytes 1081376 | tf_op jit(solution)/shard_map/all_to_all | solution.py:226
  59.2 1.5 %shard_map.48 = f32[16,2,8,128]{3,2,1,0:T(8,128)S(1)} custom-call(s32[5]{0:T(128)S(1)} %stack.32.place_ref, s32[4]{0:T(128)S(1)} %copy-done.1, s32[128,1]{1,0:T(8,128)S(1)} %copy.9.label_ref, bf16[128,4224]{1,0:T(8,128)(2,1)S(1)} %bitcast.19, bf16[2,7,160,128]{3,2,1,0:T(8,128)(2,1)S(1)} %pad_maximum_fusion.b00_ref, ...), custom_call_target="tpu_custom_call" | custom-call | tf_op jit(solution)/shard_map/pallas_call | solution.py:190
  60.7 24.1 %all_to_all.15 = f32[32,8,128]{2,1,0:T(8,128)S(1)} all-to-all(f32[32,8,128]{2,1,0:T(8,128)S(1)} %bitcast.22), channel_id=1, replica_groups=mesh['xl'=2,'z'=16,'co'=2,'xh'=2,'y'=4] {'z','xh'}, dimensions={0} | all-to-all | bytes 262144 | tf_op jit(solution)/shard_map/all_to_all | solution.py:230
  84.8 0.6 reduce_sum.29
  (2 shorter events, 0.0 us)
Async XLA Ops:
  0.0 3.6 %copy-start.1 = (s32[4]{0:T(128)S(1)}, s32[4]{0:T(128)}, u32[]{:S(2)}) copy-start(s32[4]{0:T(128)} %size_ref.5) | copy-start | bytes 52
  0.0 3.6 %copy-start.2 = (s32[50]{0:T(128)S(1)}, s32[50]{0:T(128)}, u32[]{:S(2)}) copy-start(s32[50]{0:T(128)} %occ_ref.1) | copy-start | bytes 604
  3.6 21.5 %copy-start = (bf16[2500,128]{1,0:T(8,128)(2,1)S(1)}, bf16[2500,128]{1,0:T(8,128)(2,1)}, u32[]{:S(2)}) copy-start(bf16[2500,128]{1,0:T(8,128)(2,1)} %b_ref) | copy-start | bytes 1920004
  6.2 33.6 %all-to-all-start = ((bf16[16,2,4224]{2,1,0:T(2,128)(2,1)}), bf16[16,2,4224]{2,1,0:T(2,128)(2,1)S(1)}, u32[]{:S(2)}, u32[]{:S(2)}) async-start(bf16[16,2,4224]{2,1,0:T(2,128)(2,1)} %bitcast.8), calls=%async_computation | async-start | bytes 540672 | tf_op jit(solution)/shard_map/all_to_all | solution.py:219
  25.9 11.4 %collective-permute-start = (bf16[7,160,128]{2,1,0:T(8,128)(2,1)S(1)}, bf16[7,160,128]{2,1,0:T(8,128)(2,1)S(1)}, u32[]{:S(2)}, u32[]{:S(2)}) collective-permute-start(bf16[7,160,128]{2,1,0:T(8,128)(2,1)S(1)} %shard_map.47), channel_id=1, source_target_pairs={{0,4},{4,0},{1,5},{5,1},{2,6},{6,2},{3,7},{7,3},{8,12},{12,8},{9,1... | collective-permute-start | bytes 860168 | tf_op jit(solution)/shard_map/ppermute | solution.py:211
  37.4 15.1 %collective-permute-start.2 = (bf16[2,7,160,128]{3,2,1,0:T(8,128)(2,1)S(1)}, bf16[2,7,160,128]{3,2,1,0:T(8,128)(2,1)S(1)}, u32[]{:S(2)}, u32[]{:S(2)}) collective-permute-start(bf16[2,7,160,128]{3,2,1,0:T(8,128)(2,1)S(1)} %pad_maximum_fusion.b00_ref), channel_id=1, source_target_pairs={{0,256},{256,0},{1,257},{257,1},{2,258},{258,2},{3,259},{259,3},{4... | collective-permute-start | bytes 1720328 | tf_op jit(solution)/shard_map/ppermute | solution.py:211
  41.0 18.1 %all-to-all-start.1 = ((bf16[4,32,4224]{2,1,0:T(8,128)(2,1)}), bf16[4,32,4224]{2,1,0:T(8,128)(2,1)S(1)}, u32[]{:S(2)}, u32[]{:S(2)}) async-start(bf16[4,32,4224]{2,1,0:T(8,128)(2,1)} %broadcast_in_dim.31), calls=%async_computation.1 | async-start | bytes 2162688 | tf_op jit(solution)/shard_map/all_to_all | solution.py:226
  45.5 9.2 %collective-permute-start.1 = (bf16[2,7,160,128]{3,2,1,0:T(8,128)(2,1)S(1)}, bf16[2,7,160,128]{3,2,1,0:T(8,128)(2,1)S(1)}, u32[]{:S(2)}, u32[]{:S(2)}) collective-permute-start(bf16[2,7,160,128]{3,2,1,0:T(8,128)(2,1)S(1)} %pad_maximum_fusion.b00_ref), channel_id=1, source_target_pairs={{0,8},{8,0},{1,9},{9,1},{2,10},{10,2},{3,11},{11,3},{4,12},{12,4},... | collective-permute-start | bytes 1720328 | tf_op jit(solution)/shard_map/ppermute | solution.py:211
  52.5 3.9 %collective-permute-start.3 = (bf16[2,7,160,128]{3,2,1,0:T(8,128)(2,1)S(1)}, bf16[2,7,160,128]{3,2,1,0:T(8,128)(2,1)S(1)}, u32[]{:S(2)}, u32[]{:S(2)}) collective-permute-start(bf16[2,7,160,128]{3,2,1,0:T(8,128)(2,1)S(1)} %collective-permute-done.2.b10_ref), channel_id=1, source_target_pairs={{0,8},{8,0},{1,9},{9,1},{2,10},{10,2},{3,11},{11,3},{4,12},{12,4},... | collective-permute-start | bytes 1720328 | tf_op jit(solution)/shard_map/ppermute | solution.py:211

commit v6 on v5

--- a/solution.py
+++ b/solution.py
@@ -17,6 +17,7 @@
 GROUPS = -(-TILES // 4)
 DEPTH = (TILES + GROUPS) * MAIN
 PAD = 304
+PITCH = 64
 BF16 = jnp.bfloat16
 F32 = jnp.float32
 
@@ -63,7 +64,7 @@
         out_ref[j] = jnp.where(t < length, kept, 0.0).astype(BF16)
 
 
-def pack_amplitudes(place_ref, size_ref, occ_ref, a_ref, out_ref, pick_ref, main_ref, rest_ref):
+def pack_amplitudes(place_ref, size_ref, occ_ref, a_ref, out_ref, pick_ref, main_ref, rest_ref, line_ref):
     xl, z, co, xh, y = [place_ref[i] for i in range(5)]
     starts = block_starts(size_ref)
     first = (xl * 32 + z * 2 + co) * 16 + (xh * 4 + y) * 2
@@ -74,20 +75,22 @@
         pick_ref[:, 2 * MAIN * k : 2 * MAIN * (k + 1)] = jnp.where(
             d == t + starts[k], 1.0, 0.0
         ).astype(BF16)
-    orbital = block_of(starts, lax.broadcasted_iota(jnp.int32, (VIRTUAL, 1), 0))
+    row = lax.broadcasted_iota(jnp.int32, (8 * PITCH, 1), 0)
+    orbital = block_of(starts, row % PITCH * 8 + row // PITCH)
     group = lax.broadcasted_iota(jnp.int32, (16, MAIN), 1) // REST
     for i in range(2):
         pair = first + i
         label = jnp.bitwise_xor(occ_ref[pair // OCCUPIED], occ_ref[pair % OCCUPIED])
         want = jnp.bitwise_xor(orbital, label)
-        picked = jnp.dot(
-            a_ref[i * VIRTUAL : (i + 1) * VIRTUAL], pick_ref[...], preferred_element_type=F32
-        )
-        kept = jnp.zeros((VIRTUAL, 2 * MAIN), F32)
+        for e in range(8):
+            line_ref[e * PITCH : e * PITCH + 50] = a_ref[i, :, VIRTUAL * e : VIRTUAL * (e + 1)]
+        picked = jnp.dot(line_ref[...], pick_ref[...], preferred_element_type=F32)
+        kept = jnp.zeros((8 * PITCH, 2 * MAIN), F32)
         for k in range(4):
             kept = jnp.where(want == k, picked[:, 2 * MAIN * k : 2 * MAIN * (k + 1)], kept)
-        main_ref[...] = kept[:, :MAIN]
-        rest_ref[...] = kept[:, MAIN:]
+        for e in range(8):
+            main_ref[pl.ds(e, 50, stride=8)] = kept[e * PITCH : e * PITCH + 50, :MAIN]
+            rest_ref[pl.ds(e, 50, stride=8)] = kept[e * PITCH : e * PITCH + 50, MAIN:]
         for v in range(GROUPS):
             packed = jnp.zeros((16, MAIN), F32)
             for m in range(4):
@@ -182,8 +185,9 @@
             pltpu.VMEM((VIRTUAL, 8 * MAIN), BF16),
             pltpu.VMEM((VIRTUAL, MAIN), F32),
             pltpu.VMEM((VIRTUAL, MAIN), F32),
+            pltpu.VMEM((8 * PITCH, VIRTUAL), BF16),
         ],
-    )(place, block_sizes, occ_irreps, amplitudes.reshape(2 * VIRTUAL, VIRTUAL))
+    )(place, block_sizes, occ_irreps, amplitudes.reshape(2, 50, 8 * VIRTUAL))
 
 
 def run_multiply(place, block_sizes, labels, spread, blocks):

time: 85.9 us -> 84.9 us (0.988)
  local copies, waits for them, and re-layouts: 5.77 us -> 4.49 us
    reshape x1, local copies, waits for them, and re-layouts: 3.48 us -> 2.2 us  [run_pack_amplitudes(): amplitudes.reshape(2, 50, 8 * VIRTUAL)]
where the time goes in v6:
time: 84.9 us; the launch traced here: 84.5 us
  starting transfers between devices  33.6 us (40%)
  blocking collectives  24.1 us (28%)
  waiting for transfers between devices  17 us (20%)
  local copies, waits for them, and re-layouts  4.49 us (5%)
  Pallas kernels  4.46 us (5%)
    all_to_all x1, blocking collectives, on_device(): lax.all_to_all(parts.reshape(32, 8, 128), ('z', 'xh'), split_axis=0, conc...  24.1 us
    all_to_all x1, starting transfers between devices, on_device(): lax.all_to_all(sent, 'z', split_axis=0, concat_axis=0, tiled=True, axis_i...  18.9 us
    ppermute x4, waiting for transfers between devices, swap(): return lax.ppermute(array, axis, [(0, 1), (1, 0)])  14.2 us
    ppermute x4, starting transfers between devices, swap(): return lax.ppermute(array, axis, [(0, 1), (1, 0)])  10.3 us
    all_to_all x1, starting transfers between devices, on_device(): lax.all_to_all(copies, 'y', split_axis=0, concat_axis=0, tiled=True)  4.46 us
    all_to_all x1, waiting for transfers between devices, on_device(): lax.all_to_all(copies, 'y', split_axis=0, concat_axis=0, tiled=True)  2.79 us
    reshape x1, local copies, waits for them, and re-layouts, run_pack_amplitudes(): amplitudes.reshape(2, 50, 8 * VIRTUAL)  2.2 us
    pallas_call x1, Pallas kernels, run_pack_amplitudes(): call(pack_amplitudes, (2, 16, DEPTH), BF16, in_smem(3) + in_vmem(1), [plt...  2.09 us
  transfers between devices with their start and end apart: 6, of which 4 were waited for; matrix products, arithmetic and copies ran while one was open for 2% of the time, Pallas kernels for 1%

profile of v6, /device:TPU:2, one launch (start us, length us, event | category | flops | bytes accessed | tf_op | source)
XLA Modules:
  0.0 84.5 jit_solution(16592537632726584356)
XLA Ops:
  0.0 0.0 copy-start.1
  0.0 0.0 copy-start.2
  0.0 2.2 %reshape.96.a_ref = bf16[2,50,3200]{2,1,0:T(8,128)(2,1)S(1)} reshape(bf16[2,160000]{1,0:T(2,128)(2,1)} %param.4) | data formatting | bytes 1280000 | tf_op jit(solution)/shard_map/reshape | solution.py:190
  2.2 0.0 copy-start
  2.2 0.1 stack.32.place_ref
  2.3 0.0 copy-done.1
  2.3 0.0 copy-done.2
  2.3 2.1 %shard_map.46 = bf16[2,16,4224]{2,1,0:T(8,128)(2,1)S(1)} custom-call(s32[5]{0:T(128)S(1)} %stack.32.place_ref, s32[4]{0:T(128)S(1)} %copy-done.1, s32[50]{0:T(128)S(1)} %copy-done.2, bf16[2,50,3200]{2,1,0:T(8,128)(2,1)S(1)} %reshape.96.a_ref), custom_call_target="tpu_custom_call" | custom-call | tf_op jit(solution)/shard_map/pallas_call | solution.py:179
  4.4 0.9 %copy.8 = bf16[2,2,8,4224]{3,0,1,2:T(2,128)(2,1)} copy(bf16[2,2,8,4224]{3,2,1,0:T(8,128)(2,1)S(1)} %bitcast.21) | data formatting | bytes 540672 | tf_op jit(solution)/shard_map/reshape | solution.py:221
  5.3 18.9 %all-to-all-start = ((bf16[16,2,4224]{2,1,0:T(2,128)(2,1)}), bf16[16,2,4224]{2,1,0:T(2,128)(2,1)S(1)}, u32[]{:S(2)}, u32[]{:S(2)}) async-start(bf16[16,2,4224]{2,1,0:T(2,128)(2,1)} %bitcast.8), calls=%async_computation | async-start | bytes 540672 | tf_op jit(solution)/shard_map/all_to_all | solution.py:223
  24.2 0.0 copy-done
  24.2 0.8 shard_map.47
  25.0 4.0 %collective-permute-start = (bf16[7,160,128]{2,1,0:T(8,128)(2,1)S(1)}, bf16[7,160,128]{2,1,0:T(8,128)(2,1)S(1)}, u32[]{:S(2)}, u32[]{:S(2)}) collective-permute-start(bf16[7,160,128]{2,1,0:T(8,128)(2,1)S(1)} %shard_map.47), channel_id=1, source_target_pairs={{0,4},{4,0},{1,5},{5,1},{2,6},{6,2},{3,7},{7,3},{8,12},{12,8},{9,1... | collective-permute-start | bytes 860168 | tf_op jit(solution)/shard_map/ppermute | solution.py:215
  29.1 7.4 %collective-permute-done = bf16[7,160,128]{2,1,0:T(8,128)(2,1)S(1)} collective-permute-done((bf16[7,160,128]{2,1,0:T(8,128)(2,1)S(1)}, bf16[7,160,128]{2,1,0:T(8,128)(2,1)S(1)}, u32[]{:S(2)}, u32[]{:S(2)}) %collective-permute-start) | collective-permute-done | bytes 286752 | tf_op jit(solution)/shard_map/ppermute | solution.py:215
  36.4 0.1 pad_maximum_fusion.b00_ref
  36.5 2.4 %collective-permute-start.2 = (bf16[2,7,160,128]{3,2,1,0:T(8,128)(2,1)S(1)}, bf16[2,7,160,128]{3,2,1,0:T(8,128)(2,1)S(1)}, u32[]{:S(2)}, u32[]{:S(2)}) collective-permute-start(bf16[2,7,160,128]{3,2,1,0:T(8,128)(2,1)S(1)} %pad_maximum_fusion.b00_ref), channel_id=1, source_target_pairs={{0,256},{256,0},{1,257},{257,1},{2,258},{258,2},{3,259},{259,3},{4... | collective-permute-start | bytes 1720328 | tf_op jit(solution)/shard_map/ppermute | solution.py:215
  38.9 0.0 all-to-all-done
  38.9 0.1 broadcast_in_dim.30
  39.1 1.1 %broadcast_in_dim.31 = bf16[4,32,4224]{2,1,0:T(8,128)(2,1)} broadcast(bf16[32,4224]{1,0:T(8,128)(2,1)S(1)} %broadcast_in_dim.30), dimensions={1,2} | broadcast | bytes 1351680 | tf_op jit(solution)/shard_map/broadcast_in_dim | solution.py:229
  40.1 4.5 %all-to-all-start.1 = ((bf16[4,32,4224]{2,1,0:T(8,128)(2,1)}), bf16[4,32,4224]{2,1,0:T(8,128)(2,1)S(1)}, u32[]{:S(2)}, u32[]{:S(2)}) async-start(bf16[4,32,4224]{2,1,0:T(8,128)(2,1)} %broadcast_in_dim.31), calls=%async_computation.1 | async-start | bytes 2162688 | tf_op jit(solution)/shard_map/all_to_all | solution.py:230
  44.6 1.9 %collective-permute-start.1 = (bf16[2,7,160,128]{3,2,1,0:T(8,128)(2,1)S(1)}, bf16[2,7,160,128]{3,2,1,0:T(8,128)(2,1)S(1)}, u32[]{:S(2)}, u32[]{:S(2)}) collective-permute-start(bf16[2,7,160,128]{3,2,1,0:T(8,128)(2,1)S(1)} %pad_maximum_fusion.b00_ref), channel_id=1, source_target_pairs={{0,8},{8,0},{1,9},{9,1},{2,10},{10,2},{3,11},{11,3},{4,12},{12,4},... | collective-permute-start | bytes 1720328 | tf_op jit(solution)/shard_map/ppermute | solution.py:215
  46.5 5.1 %collective-permute-done.2.b10_ref = bf16[2,7,160,128]{3,2,1,0:T(8,128)(2,1)S(1)} collective-permute-done((bf16[2,7,160,128]{3,2,1,0:T(8,128)(2,1)S(1)}, bf16[2,7,160,128]{3,2,1,0:T(8,128)(2,1)S(1)}, u32[]{:S(2)}, u32[]{:S(2)}) %collective-permute-start.2) | collective-permute-done | bytes 573472 | tf_op jit(solution)/shard_map/ppermute | solution.py:215
  51.6 1.9 %collective-permute-start.3 = (bf16[2,7,160,128]{3,2,1,0:T(8,128)(2,1)S(1)}, bf16[2,7,160,128]{3,2,1,0:T(8,128)(2,1)S(1)}, u32[]{:S(2)}, u32[]{:S(2)}) collective-permute-start(bf16[2,7,160,128]{3,2,1,0:T(8,128)(2,1)S(1)} %collective-permute-done.2.b10_ref), channel_id=1, source_target_pairs={{0,8},{8,0},{1,9},{9,1},{2,10},{10,2},{3,11},{11,3},{4,12},{12,4},... | collective-permute-start | bytes 1720328 | tf_op jit(solution)/shard_map/ppermute | solution.py:215
  53.6 0.1 select_reduce_fusion
  53.7 0.1 copy.9.label_ref
  53.8 0.0 collective-permute-done.1.b01_ref
  53.8 1.7 %collective-permute-done.3.b11_ref = bf16[2,7,160,128]{3,2,1,0:T(8,128)(2,1)S(1)} collective-permute-done((bf16[2,7,160,128]{3,2,1,0:T(8,128)(2,1)S(1)}, bf16[2,7,160,128]{3,2,1,0:T(8,128)(2,1)S(1)}, u32[]{:S(2)}, u32[]{:S(2)}) %collective-permute-start.3) | collective-permute-done | bytes 573472 | tf_op jit(solution)/shard_map/ppermute | solution.py:215
  55.5 2.8 %all-to-all-done.1 = bf16[4,32,4224]{2,1,0:T(8,128)(2,1)S(1)} async-done(((bf16[4,32,4224]{2,1,0:T(8,128)(2,1)}), bf16[4,32,4224]{2,1,0:T(8,128)(2,1)S(1)}, u32[]{:S(2)}, u32[]{:S(2)}) %all-to-all-start.1) | async-done | bytes 1081376 | tf_op jit(solution)/shard_map/all_to_all | solution.py:230
  58.3 1.5 %shard_map.48 = f32[16,2,8,128]{3,2,1,0:T(8,128)S(1)} custom-call(s32[5]{0:T(128)S(1)} %stack.32.place_ref, s32[4]{0:T(128)S(1)} %copy-done.1, s32[128,1]{1,0:T(8,128)S(1)} %copy.9.label_ref, bf16[128,4224]{1,0:T(8,128)(2,1)S(1)} %bitcast.19, bf16[2,7,160,128]{3,2,1,0:T(8,128)(2,1)S(1)} %pad_maximum_fusion.b00_ref, ...), custom_call_target="tpu_custom_call" | custom-call | tf_op jit(solution)/shard_map/pallas_call | solution.py:194
  59.8 24.1 %all_to_all.15 = f32[32,8,128]{2,1,0:T(8,128)S(1)} all-to-all(f32[32,8,128]{2,1,0:T(8,128)S(1)} %bitcast.22), channel_id=1, replica_groups=mesh['xl'=2,'z'=16,'co'=2,'xh'=2,'y'=4] {'z','xh'}, dimensions={0} | all-to-all | bytes 262144 | tf_op jit(solution)/shard_map/all_to_all | solution.py:234
  83.9 0.6 reduce_sum.29
  (2 shorter events, 0.0 us)
Async XLA Ops:
  0.0 2.3 %copy-start.1 = (s32[4]{0:T(128)S(1)}, s32[4]{0:T(128)}, u32[]{:S(2)}) copy-start(s32[4]{0:T(128)} %size_ref.5) | copy-start | bytes 52
  0.0 2.3 %copy-start.2 = (s32[50]{0:T(128)S(1)}, s32[50]{0:T(128)}, u32[]{:S(2)}) copy-start(s32[50]{0:T(128)} %occ_ref.1) | copy-start | bytes 604
  2.2 22.0 %copy-start = (bf16[2500,128]{1,0:T(8,128)(2,1)S(1)}, bf16[2500,128]{1,0:T(8,128)(2,1)}, u32[]{:S(2)}) copy-start(bf16[2500,128]{1,0:T(8,128)(2,1)} %b_ref) | copy-start | bytes 1920004
  5.3 33.6 %all-to-all-start = ((bf16[16,2,4224]{2,1,0:T(2,128)(2,1)}), bf16[16,2,4224]{2,1,0:T(2,128)(2,1)S(1)}, u32[]{:S(2)}, u32[]{:S(2)}) async-start(bf16[16,2,4224]{2,1,0:T(2,128)(2,1)} %bitcast.8), calls=%async_computation | async-start | bytes 540672 | tf_op jit(solution)/shard_map/all_to_all | solution.py:223
  25.0 11.4 %collective-permute-start = (bf16[7,160,128]{2,1,0:T(8,128)(2,1)S(1)}, bf16[7,160,128]{2,1,0:T(8,128)(2,1)S(1)}, u32[]{:S(2)}, u32[]{:S(2)}) collective-permute-start(bf16[7,160,128]{2,1,0:T(8,128)(2,1)S(1)} %shard_map.47), channel_id=1, source_target_pairs={{0,4},{4,0},{1,5},{5,1},{2,6},{6,2},{3,7},{7,3},{8,12},{12,8},{9,1... | collective-permute-start | bytes 860168 | tf_op jit(solution)/shard_map/ppermute | solution.py:215
  36.5 15.1 %collective-permute-start.2 = (bf16[2,7,160,128]{3,2,1,0:T(8,128)(2,1)S(1)}, bf16[2,7,160,128]{3,2,1,0:T(8,128)(2,1)S(1)}, u32[]{:S(2)}, u32[]{:S(2)}) collective-permute-start(bf16[2,7,160,128]{3,2,1,0:T(8,128)(2,1)S(1)} %pad_maximum_fusion.b00_ref), channel_id=1, source_target_pairs={{0,256},{256,0},{1,257},{257,1},{2,258},{258,2},{3,259},{259,3},{4... | collective-permute-start | bytes 1720328 | tf_op jit(solution)/shard_map/ppermute | solution.py:215
  40.1 18.1 %all-to-all-start.1 = ((bf16[4,32,4224]{2,1,0:T(8,128)(2,1)}), bf16[4,32,4224]{2,1,0:T(8,128)(2,1)S(1)}, u32[]{:S(2)}, u32[]{:S(2)}) async-start(bf16[4,32,4224]{2,1,0:T(8,128)(2,1)} %broadcast_in_dim.31), calls=%async_computation.1 | async-start | bytes 2162688 | tf_op jit(solution)/shard_map/all_to_all | solution.py:230
  44.6 9.2 %collective-permute-start.1 = (bf16[2,7,160,128]{3,2,1,0:T(8,128)(2,1)S(1)}, bf16[2,7,160,128]{3,2,1,0:T(8,128)(2,1)S(1)}, u32[]{:S(2)}, u32[]{:S(2)}) collective-permute-start(bf16[2,7,160,128]{3,2,1,0:T(8,128)(2,1)S(1)} %pad_maximum_fusion.b00_ref), channel_id=1, source_target_pairs={{0,8},{8,0},{1,9},{9,1},{2,10},{10,2},{3,11},{11,3},{4,12},{12,4},... | collective-permute-start | bytes 1720328 | tf_op jit(solution)/shard_map/ppermute | solution.py:215
  51.6 3.9 %collective-permute-start.3 = (bf16[2,7,160,128]{3,2,1,0:T(8,128)(2,1)S(1)}, bf16[2,7,160,128]{3,2,1,0:T(8,128)(2,1)S(1)}, u32[]{:S(2)}, u32[]{:S(2)}) collective-permute-start(bf16[2,7,160,128]{3,2,1,0:T(8,128)(2,1)S(1)} %collective-permute-done.2.b10_ref), channel_id=1, source_target_pairs={{0,8},{8,0},{1,9},{9,1},{2,10},{10,2},{3,11},{11,3},{4,12},{12,4},... | collective-permute-start | bytes 1720328 | tf_op jit(solution)/shard_map/ppermute | solution.py:215

commit v7 on v6

--- a/solution.py
+++ b/solution.py
@@ -18,6 +18,7 @@
 DEPTH = (TILES + GROUPS) * MAIN
 PAD = 304
 PITCH = 64
+HEAD = SEGMENTS * MAIN
 BF16 = jnp.bfloat16
 F32 = jnp.float32
 
@@ -61,7 +62,9 @@
             rows = pad_ref[pl.ds(PAD - offset + VIRTUAL * j + starts[k], WIDTH), :]
             kept = jnp.where(want == k, rows, kept)
             length = jnp.where(want == k, size_ref[k], length)
-        out_ref[j] = jnp.where(t < length, kept, 0.0).astype(BF16)
+        kept = jnp.where(t < length, kept, 0.0).astype(BF16)
+        out_ref[MAIN * j : MAIN * (j + 1)] = kept[:MAIN]
+        out_ref[HEAD + REST * j : HEAD + REST * (j + 1)] = kept[MAIN:]
 
 
 def pack_amplitudes(place_ref, size_ref, occ_ref, a_ref, out_ref, pick_ref, main_ref, rest_ref, line_ref):
@@ -107,31 +110,32 @@
             out_ref[i, :, lo : lo + MAIN] = packed.astype(BF16)
 
 
-def multiply(place_ref, size_ref, label_ref, a_ref, b00_ref, b01_ref, b10_ref, b11_ref, out_ref, b_ref, sum_ref):
+def multiply(place_ref, size_ref, label_ref, a_ref, b00_ref, b01_ref, b10_ref, b11_ref, out_ref, rest_ref, sum_ref):
     xl, z, co, xh, y = [place_ref[i] for i in range(5)]
     starts = block_starts(size_ref)
     low = TILES * MAIN
-    spare = DEPTH - low - TILES * REST
-    b_ref[low + TILES * REST :] = jnp.zeros((spare, 256), BF16)
+    rest_ref[TILES * REST :] = jnp.zeros((DEPTH - low - TILES * REST, 256), BF16)
     for w in (0, 6, 12, 13, 19, 25):
-        b_ref[w * MAIN : (w + 1) * MAIN] = jnp.zeros((MAIN, 256), BF16)
-        b_ref[low + w * REST : low + (w + 1) * REST] = jnp.zeros((REST, 256), BF16)
+        rest_ref[w * REST : (w + 1) * REST] = jnp.zeros((REST, 256), BF16)
+    totals = [jnp.zeros((128, 128), F32), jnp.zeros((128, 128), F32)]
     for flip_co, refs in ((0, (b00_ref, b10_ref)), (1, (b01_ref, b11_ref))):
         for flip_xl, from_ref in enumerate(refs):
             base = jnp.bitwise_xor(xl, flip_xl) * WINDOWS + jnp.bitwise_xor(co, flip_co) * 6
+            left = a_ref[:, pl.ds(pl.multiple_of(base * MAIN, MAIN), HEAD)]
             for flip_xh in range(2):
+                totals[flip_xh] += jnp.dot(
+                    left, from_ref[flip_xh, 0:HEAD], preferred_element_type=F32
+                )
                 lanes = slice(flip_xh * 128, (flip_xh + 1) * 128)
                 for j in range(SEGMENTS):
-                    upper = pl.ds(pl.multiple_of((base + j) * MAIN, MAIN), MAIN)
-                    lower = pl.ds(pl.multiple_of(low + (base + j) * REST, REST), REST)
-                    head = from_ref[flip_xh, j, 0:MAIN]
-                    tail = from_ref[flip_xh, j, MAIN:WIDTH]
+                    lower = pl.ds(pl.multiple_of((base + j) * REST, REST), REST)
+                    tail = from_ref[flip_xh, HEAD + REST * j : HEAD + REST * (j + 1)]
                     if j in (0, 6):
-                        head = head + b_ref[upper, lanes]
-                        tail = tail + b_ref[lower, lanes]
-                    b_ref[upper, lanes] = head
-                    b_ref[lower, lanes] = tail
-    total = jnp.dot(a_ref[...], b_ref[...], preferred_element_type=F32)
+                        tail = tail + rest_ref[lower, lanes]
+                    rest_ref[lower, lanes] = tail
+    total = jnp.concatenate(totals, 1) + jnp.dot(
+        a_ref[:, low:], rest_ref[...], preferred_element_type=F32
+    )
     for flip_xh in range(2):
         there = jnp.bitwise_xor(xh, flip_xh)
         label = column_label(starts, (there * 4 + y) * 128)
@@ -168,7 +172,7 @@
 def run_pack_integrals(place, block_sizes, integrals):
     return call(
         pack_integrals,
-        (SEGMENTS, WIDTH, 128),
+        (SEGMENTS * WIDTH, 128),
         BF16,
         in_smem(2) + in_vmem(1),
         [pltpu.VMEM((PAD + SEGMENTS * VIRTUAL + WIDTH, 128), F32)],
@@ -196,7 +200,7 @@
         (16, 2, 8, 128),
         F32,
         in_smem(2) + in_vmem(6),
-        [pltpu.VMEM((DEPTH, 256), BF16), pltpu.VMEM((128, 128), F32)],
+        [pltpu.VMEM((DEPTH - TILES * MAIN, 256), BF16), pltpu.VMEM((128, 128), F32)],
     )(place, block_sizes, labels, spread, *blocks)
 
 

time: 84.9 us -> 84.7 us (level)
  no operation moved by 1% of the time
where the time goes in v7:
time: 84.7 us; the launch traced here: 84.3 us
  starting transfers between devices  33.6 us (40%)
  blocking collectives  24.1 us (28%)
  waiting for transfers between devices  17 us (20%)
  local copies, waits for them, and re-layouts  4.49 us (5%)
  Pallas kernels  4.24 us (5%)
    all_to_all x1, blocking collectives, on_device(): lax.all_to_all(parts.reshape(32, 8, 128), ('z', 'xh'), split_axis=0, conc...  24.1 us
    all_to_all x1, starting transfers between devices, on_device(): lax.all_to_all(sent, 'z', split_axis=0, concat_axis=0, tiled=True, axis_i...  18.9 us
    ppermute x4, waiting for transfers between devices, swap(): return lax.ppermute(array, axis, [(0, 1), (1, 0)])  14.2 us
    ppermute x4, starting transfers between devices, swap(): return lax.ppermute(array, axis, [(0, 1), (1, 0)])  10.3 us
    all_to_all x1, starting transfers between devices, on_device(): lax.all_to_all(copies, 'y', split_axis=0, concat_axis=0, tiled=True)  4.46 us
    all_to_all x1, waiting for transfers between devices, on_device(): lax.all_to_all(copies, 'y', split_axis=0, concat_axis=0, tiled=True)  2.79 us
    reshape x1, local copies, waits for them, and re-layouts, run_pack_amplitudes(): amplitudes.reshape(2, 50, 8 * VIRTUAL)  2.2 us
    pallas_call x1, Pallas kernels, run_pack_amplitudes(): call(pack_amplitudes, (2, 16, DEPTH), BF16, in_smem(3) + in_vmem(1), [plt...  2.09 us
  transfers between devices with their start and end apart: 6, of which 4 were waited for; matrix products, arithmetic and copies ran while one was open for 2% of the time, Pallas kernels for 1%

profile of v7, /device:TPU:2, one launch (start us, length us, event | category | flops | bytes accessed | tf_op | source)
XLA Modules:
  0.0 84.3 jit_solution(3238431399765933949)
XLA Ops:
  0.0 0.0 copy-start.1
  0.0 0.0 copy-start.2
  0.0 2.2 %reshape.96.a_ref = bf16[2,50,3200]{2,1,0:T(8,128)(2,1)S(1)} reshape(bf16[2,160000]{1,0:T(2,128)(2,1)} %param.4) | data formatting | bytes 1280000 | tf_op jit(solution)/shard_map/reshape | solution.py:194
  2.2 0.0 copy-start
  2.2 0.1 stack.32.place_ref
  2.3 0.0 copy-done.1
  2.3 0.0 copy-done.2
  2.3 2.1 %shard_map.46 = bf16[2,16,4224]{2,1,0:T(8,128)(2,1)S(1)} custom-call(s32[5]{0:T(128)S(1)} %stack.32.place_ref, s32[4]{0:T(128)S(1)} %copy-done.1, s32[50]{0:T(128)S(1)} %copy-done.2, bf16[2,50,3200]{2,1,0:T(8,128)(2,1)S(1)} %reshape.96.a_ref), custom_call_target="tpu_custom_call" | custom-call | tf_op jit(solution)/shard_map/pallas_call | solution.py:183
  4.4 0.9 %copy.8 = bf16[2,2,8,4224]{3,0,1,2:T(2,128)(2,1)} copy(bf16[2,2,8,4224]{3,2,1,0:T(8,128)(2,1)S(1)} %bitcast.21) | data formatting | bytes 540672 | tf_op jit(solution)/shard_map/reshape | solution.py:225
  5.3 18.9 %all-to-all-start = ((bf16[16,2,4224]{2,1,0:T(2,128)(2,1)}), bf16[16,2,4224]{2,1,0:T(2,128)(2,1)S(1)}, u32[]{:S(2)}, u32[]{:S(2)}) async-start(bf16[16,2,4224]{2,1,0:T(2,128)(2,1)} %bitcast.8), calls=%async_computation | async-start | bytes 540672 | tf_op jit(solution)/shard_map/all_to_all | solution.py:227
  24.2 0.0 copy-done
  24.2 0.8 shard_map.47
  25.0 4.0 %collective-permute-start = (bf16[1120,128]{1,0:T(8,128)(2,1)S(1)}, bf16[1120,128]{1,0:T(8,128)(2,1)S(1)}, u32[]{:S(2)}, u32[]{:S(2)}) collective-permute-start(bf16[1120,128]{1,0:T(8,128)(2,1)S(1)} %shard_map.47), channel_id=1, source_target_pairs={{0,4},{4,0},{1,5},{5,1},{2,6},{6,2},{3,7},{7,3},{8,12},{12,8},{9,1... | collective-permute-start | bytes 860168 | tf_op jit(solution)/shard_map/ppermute | solution.py:219
  29.1 7.4 %collective-permute-done = bf16[1120,128]{1,0:T(8,128)(2,1)S(1)} collective-permute-done((bf16[1120,128]{1,0:T(8,128)(2,1)S(1)}, bf16[1120,128]{1,0:T(8,128)(2,1)S(1)}, u32[]{:S(2)}, u32[]{:S(2)}) %collective-permute-start) | collective-permute-done | bytes 286752 | tf_op jit(solution)/shard_map/ppermute | solution.py:219
  36.4 0.1 pad_maximum_fusion.b00_ref
  36.5 2.4 %collective-permute-start.2 = (bf16[2,1120,128]{2,1,0:T(8,128)(2,1)S(1)}, bf16[2,1120,128]{2,1,0:T(8,128)(2,1)S(1)}, u32[]{:S(2)}, u32[]{:S(2)}) collective-permute-start(bf16[2,1120,128]{2,1,0:T(8,128)(2,1)S(1)} %pad_maximum_fusion.b00_ref), channel_id=1, source_target_pairs={{0,256},{256,0},{1,257},{257,1},{2,258},{258,2},{3,259},{259,3},{4... | collective-permute-start | bytes 1720328 | tf_op jit(solution)/shard_map/ppermute | solution.py:219
  38.9 0.0 all-to-all-done
  38.9 0.1 broadcast_in_dim.30
  39.1 1.1 %broadcast_in_dim.31 = bf16[4,32,4224]{2,1,0:T(8,128)(2,1)} broadcast(bf16[32,4224]{1,0:T(8,128)(2,1)S(1)} %broadcast_in_dim.30), dimensions={1,2} | broadcast | bytes 1351680 | tf_op jit(solution)/shard_map/broadcast_in_dim | solution.py:233
  40.1 4.5 %all-to-all-start.1 = ((bf16[4,32,4224]{2,1,0:T(8,128)(2,1)}), bf16[4,32,4224]{2,1,0:T(8,128)(2,1)S(1)}, u32[]{:S(2)}, u32[]{:S(2)}) async-start(bf16[4,32,4224]{2,1,0:T(8,128)(2,1)} %broadcast_in_dim.31), calls=%async_computation.1 | async-start | bytes 2162688 | tf_op jit(solution)/shard_map/all_to_all | solution.py:234
  44.6 1.9 %collective-permute-start.1 = (bf16[2,1120,128]{2,1,0:T(8,128)(2,1)S(1)}, bf16[2,1120,128]{2,1,0:T(8,128)(2,1)S(1)}, u32[]{:S(2)}, u32[]{:S(2)}) collective-permute-start(bf16[2,1120,128]{2,1,0:T(8,128)(2,1)S(1)} %pad_maximum_fusion.b00_ref), channel_id=1, source_target_pairs={{0,8},{8,0},{1,9},{9,1},{2,10},{10,2},{3,11},{11,3},{4,12},{12,4},... | collective-permute-start | bytes 1720328 | tf_op jit(solution)/shard_map/ppermute | solution.py:219
  46.5 5.1 %collective-permute-done.2.b10_ref = bf16[2,1120,128]{2,1,0:T(8,128)(2,1)S(1)} collective-permute-done((bf16[2,1120,128]{2,1,0:T(8,128)(2,1)S(1)}, bf16[2,1120,128]{2,1,0:T(8,128)(2,1)S(1)}, u32[]{:S(2)}, u32[]{:S(2)}) %collective-permute-start.2) | collective-permute-done | bytes 573472 | tf_op jit(solution)/shard_map/ppermute | solution.py:219
  51.6 1.9 %collective-permute-start.3 = (bf16[2,1120,128]{2,1,0:T(8,128)(2,1)S(1)}, bf16[2,1120,128]{2,1,0:T(8,128)(2,1)S(1)}, u32[]{:S(2)}, u32[]{:S(2)}) collective-permute-start(bf16[2,1120,128]{2,1,0:T(8,128)(2,1)S(1)} %collective-permute-done.2.b10_ref), channel_id=1, source_target_pairs={{0,8},{8,0},{1,9},{9,1},{2,10},{10,2},{3,11},{11,3},{4,12},{12,4},... | collective-permute-start | bytes 1720328 | tf_op jit(solution)/shard_map/ppermute | solution.py:219
  53.6 0.1 select_reduce_fusion
  53.7 0.1 copy.9.label_ref
  53.8 0.0 collective-permute-done.1.b01_ref
  53.8 1.7 %collective-permute-done.3.b11_ref = bf16[2,1120,128]{2,1,0:T(8,128)(2,1)S(1)} collective-permute-done((bf16[2,1120,128]{2,1,0:T(8,128)(2,1)S(1)}, bf16[2,1120,128]{2,1,0:T(8,128)(2,1)S(1)}, u32[]{:S(2)}, u32[]{:S(2)}) %collective-permute-start.3) | collective-permute-done | bytes 573472 | tf_op jit(solution)/shard_map/ppermute | solution.py:219
  55.5 2.8 %all-to-all-done.1 = bf16[4,32,4224]{2,1,0:T(8,128)(2,1)S(1)} async-done(((bf16[4,32,4224]{2,1,0:T(8,128)(2,1)}), bf16[4,32,4224]{2,1,0:T(8,128)(2,1)S(1)}, u32[]{:S(2)}, u32[]{:S(2)}) %all-to-all-start.1) | async-done | bytes 1081376 | tf_op jit(solution)/shard_map/all_to_all | solution.py:234
  58.3 1.3 %shard_map.48 = f32[16,2,8,128]{3,2,1,0:T(8,128)S(1)} custom-call(s32[5]{0:T(128)S(1)} %stack.32.place_ref, s32[4]{0:T(128)S(1)} %copy-done.1, s32[128,1]{1,0:T(8,128)S(1)} %copy.9.label_ref, bf16[128,4224]{1,0:T(8,128)(2,1)S(1)} %bitcast.19, bf16[2,1120,128]{2,1,0:T(8,128)(2,1)S(1)} %pad_maximum_fusion.b00_ref, ...), custom_call_target="tpu_custom_call" | custom-call | tf_op jit(solution)/shard_map/pallas_call | solution.py:198
  59.6 24.1 %all_to_all.15 = f32[32,8,128]{2,1,0:T(8,128)S(1)} all-to-all(f32[32,8,128]{2,1,0:T(8,128)S(1)} %bitcast.22), channel_id=1, replica_groups=mesh['xl'=2,'z'=16,'co'=2,'xh'=2,'y'=4] {'z','xh'}, dimensions={0} | all-to-all | bytes 262144 | tf_op jit(solution)/shard_map/all_to_all | solution.py:238
  83.7 0.6 reduce_sum.29
  (2 shorter events, 0.0 us)
Async XLA Ops:
  0.0 2.3 %copy-start.1 = (s32[4]{0:T(128)S(1)}, s32[4]{0:T(128)}, u32[]{:S(2)}) copy-start(s32[4]{0:T(128)} %size_ref.5) | copy-start | bytes 52
  0.0 2.3 %copy-start.2 = (s32[50]{0:T(128)S(1)}, s32[50]{0:T(128)}, u32[]{:S(2)}) copy-start(s32[50]{0:T(128)} %occ_ref.1) | copy-start | bytes 604
  2.2 22.0 %copy-start = (bf16[2500,128]{1,0:T(8,128)(2,1)S(1)}, bf16[2500,128]{1,0:T(8,128)(2,1)}, u32[]{:S(2)}) copy-start(bf16[2500,128]{1,0:T(8,128)(2,1)} %b_ref) | copy-start | bytes 1920004
  5.3 33.6 %all-to-all-start = ((bf16[16,2,4224]{2,1,0:T(2,128)(2,1)}), bf16[16,2,4224]{2,1,0:T(2,128)(2,1)S(1)}, u32[]{:S(2)}, u32[]{:S(2)}) async-start(bf16[16,2,4224]{2,1,0:T(2,128)(2,1)} %bitcast.8), calls=%async_computation | async-start | bytes 540672 | tf_op jit(solution)/shard_map/all_to_all | solution.py:227
  25.0 11.4 %collective-permute-start = (bf16[1120,128]{1,0:T(8,128)(2,1)S(1)}, bf16[1120,128]{1,0:T(8,128)(2,1)S(1)}, u32[]{:S(2)}, u32[]{:S(2)}) collective-permute-start(bf16[1120,128]{1,0:T(8,128)(2,1)S(1)} %shard_map.47), channel_id=1, source_target_pairs={{0,4},{4,0},{1,5},{5,1},{2,6},{6,2},{3,7},{7,3},{8,12},{12,8},{9,1... | collective-permute-start | bytes 860168 | tf_op jit(solution)/shard_map/ppermute | solution.py:219
  36.5 15.1 %collective-permute-start.2 = (bf16[2,1120,128]{2,1,0:T(8,128)(2,1)S(1)}, bf16[2,1120,128]{2,1,0:T(8,128)(2,1)S(1)}, u32[]{:S(2)}, u32[]{:S(2)}) collective-permute-start(bf16[2,1120,128]{2,1,0:T(8,128)(2,1)S(1)} %pad_maximum_fusion.b00_ref), channel_id=1, source_target_pairs={{0,256},{256,0},{1,257},{257,1},{2,258},{258,2},{3,259},{259,3},{4... | collective-permute-start | bytes 1720328 | tf_op jit(solution)/shard_map/ppermute | solution.py:219
  40.1 18.1 %all-to-all-start.1 = ((bf16[4,32,4224]{2,1,0:T(8,128)(2,1)}), bf16[4,32,4224]{2,1,0:T(8,128)(2,1)S(1)}, u32[]{:S(2)}, u32[]{:S(2)}) async-start(bf16[4,32,4224]{2,1,0:T(8,128)(2,1)} %broadcast_in_dim.31), calls=%async_computation.1 | async-start | bytes 2162688 | tf_op jit(solution)/shard_map/all_to_all | solution.py:234
  44.6 9.2 %collective-permute-start.1 = (bf16[2,1120,128]{2,1,0:T(8,128)(2,1)S(1)}, bf16[2,1120,128]{2,1,0:T(8,128)(2,1)S(1)}, u32[]{:S(2)}, u32[]{:S(2)}) collective-permute-start(bf16[2,1120,128]{2,1,0:T(8,128)(2,1)S(1)} %pad_maximum_fusion.b00_ref), channel_id=1, source_target_pairs={{0,8},{8,0},{1,9},{9,1},{2,10},{10,2},{3,11},{11,3},{4,12},{12,4},... | collective-permute-start | bytes 1720328 | tf_op jit(solution)/shard_map/ppermute | solution.py:219
  51.6 3.9 %collective-permute-start.3 = (bf16[2,1120,128]{2,1,0:T(8,128)(2,1)S(1)}, bf16[2,1120,128]{2,1,0:T(8,128)(2,1)S(1)}, u32[]{:S(2)}, u32[]{:S(2)}) collective-permute-start(bf16[2,1120,128]{2,1,0:T(8,128)(2,1)S(1)} %collective-permute-done.2.b10_ref), channel_id=1, source_target_pairs={{0,8},{8,0},{1,9},{9,1},{2,10},{10,2},{3,11},{11,3},{4,12},{12,4},... | collective-permute-start | bytes 1720328 | tf_op jit(solution)/shard_map/ppermute | solution.py:219

commit v8 on v7

--- a/solution.py
+++ b/solution.py
@@ -142,12 +142,10 @@
         part = jnp.where(
             label_ref[...] == label, total[:, flip_xh * 128 : (flip_xh + 1) * 128], 0.0
         )
-        sum_ref[...] = part
-        for yy in range(4):
-            for zz in range(16):
-                out_ref[(zz + 8) % 16, there, 2 * yy : 2 * yy + 2] = sum_ref[
-                    32 * yy + 2 * zz : 32 * yy + 2 * zz + 2
-                ]
+        sum_ref[0:128] = part
+        for zz in range(16):
+            pieces = [sum_ref[32 * yy + 2 * zz : 32 * yy + 2 * zz + 2] for yy in range(4)]
+            out_ref[(zz + 8) % 16, there] = jnp.concatenate(pieces, 0)
 
 
 def in_vmem(count):
@@ -187,8 +185,8 @@
         in_smem(3) + in_vmem(1),
         [
             pltpu.VMEM((VIRTUAL, 8 * MAIN), BF16),
-            pltpu.VMEM((VIRTUAL, MAIN), F32),
-            pltpu.VMEM((VIRTUAL, MAIN), F32),
+            pltpu.VMEM((512, MAIN), F32),
+            pltpu.VMEM((512, MAIN), F32),
             pltpu.VMEM((8 * PITCH, VIRTUAL), BF16),
         ],
     )(place, block_sizes, occ_irreps, amplitudes.reshape(2, 50, 8 * VIRTUAL))
@@ -200,7 +198,7 @@
         (16, 2, 8, 128),
         F32,
         in_smem(2) + in_vmem(6),
-        [pltpu.VMEM((DEPTH - TILES * MAIN, 256), BF16), pltpu.VMEM((128, 128), F32)],
+        [pltpu.VMEM((DEPTH - TILES * MAIN, 256), BF16), pltpu.VMEM((136, 128), F32)],
     )(place, block_sizes, labels, spread, *blocks)
 
 

time: 84.7 us -> 84.7 us (level)
  the two profiles are of different devices: /device:TPU:2 before, /device:TPU:8 now
where the time goes in v8:
time: 84.7 us; the launch traced here: 84.3 us
  starting transfers between devices  35.9 us (42%)
  blocking collectives  24.2 us (29%)
  waiting for transfers between devices  14.6 us (17%)
  local copies, waits for them, and re-layouts  4.49 us (5%)
  Pallas kernels  4.25 us (5%)
    all_to_all x1, blocking collectives, on_device(): lax.all_to_all(parts.reshape(32, 8, 128), ('z', 'xh'), split_axis=0, conc...  24.2 us
    all_to_all x1, starting transfers between devices, on_device(): lax.all_to_all(sent, 'z', split_axis=0, concat_axis=0, tiled=True, axis_i...  18.9 us
    ppermute x4, starting transfers between devices, swap(): return lax.ppermute(array, axis, [(0, 1), (1, 0)])  12.1 us
    ppermute x4, waiting for transfers between devices, swap(): return lax.ppermute(array, axis, [(0, 1), (1, 0)])  11.9 us
    all_to_all x1, starting transfers between devices, on_device(): lax.all_to_all(copies, 'y', split_axis=0, concat_axis=0, tiled=True)  4.91 us
    all_to_all x1, waiting for transfers between devices, on_device(): lax.all_to_all(copies, 'y', split_axis=0, concat_axis=0, tiled=True)  2.73 us
    reshape x1, local copies, waits for them, and re-layouts, run_pack_amplitudes(): amplitudes.reshape(2, 50, 8 * VIRTUAL)  2.2 us
    pallas_call x1, Pallas kernels, run_pack_amplitudes(): call(pack_amplitudes, (2, 16, DEPTH), BF16, in_smem(3) + in_vmem(1), [plt...  2.09 us
  transfers between devices with their start and end apart: 6, of which 4 were waited for; matrix products, arithmetic and copies ran while one was open for 2% of the time, Pallas kernels for 1%

profile of v8, /device:TPU:8, one launch (start us, length us, event | category | flops | bytes accessed | tf_op | source)
XLA Modules:
  0.0 84.3 jit_solution(15219552427830086764)
XLA Ops:
  0.0 0.0 copy-start.1
  0.0 0.0 copy-start.2
  0.0 2.2 %reshape.96.a_ref = bf16[2,50,3200]{2,1,0:T(8,128)(2,1)S(1)} reshape(bf16[2,160000]{1,0:T(2,128)(2,1)} %param.4) | data formatting | bytes 1280000 | tf_op jit(solution)/shard_map/reshape | solution.py:192
  2.2 0.0 copy-start
  2.2 0.1 stack.32.place_ref
  2.3 0.0 copy-done.1
  2.3 0.0 copy-done.2
  2.3 2.1 %shard_map.46 = bf16[2,16,4224]{2,1,0:T(8,128)(2,1)S(1)} custom-call(s32[5]{0:T(128)S(1)} %stack.32.place_ref, s32[4]{0:T(128)S(1)} %copy-done.1, s32[50]{0:T(128)S(1)} %copy-done.2, bf16[2,50,3200]{2,1,0:T(8,128)(2,1)S(1)} %reshape.96.a_ref), custom_call_target="tpu_custom_call" | custom-call | tf_op jit(solution)/shard_map/pallas_call | solution.py:181
  4.4 0.9 %copy.8 = bf16[2,2,8,4224]{3,0,1,2:T(2,128)(2,1)} copy(bf16[2,2,8,4224]{3,2,1,0:T(8,128)(2,1)S(1)} %bitcast.21) | data formatting | bytes 540672 | tf_op jit(solution)/shard_map/reshape | solution.py:223
  5.3 18.9 %all-to-all-start = ((bf16[16,2,4224]{2,1,0:T(2,128)(2,1)}), bf16[16,2,4224]{2,1,0:T(2,128)(2,1)S(1)}, u32[]{:S(2)}, u32[]{:S(2)}) async-start(bf16[16,2,4224]{2,1,0:T(2,128)(2,1)} %bitcast.8), calls=%async_computation | async-start | bytes 540672 | tf_op jit(solution)/shard_map/all_to_all | solution.py:225
  24.2 0.0 copy-done
  24.2 0.8 shard_map.47
  25.0 4.9 %collective-permute-start = (bf16[1120,128]{1,0:T(8,128)(2,1)S(1)}, bf16[1120,128]{1,0:T(8,128)(2,1)S(1)}, u32[]{:S(2)}, u32[]{:S(2)}) collective-permute-start(bf16[1120,128]{1,0:T(8,128)(2,1)S(1)} %shard_map.47), channel_id=1, source_target_pairs={{0,4},{4,0},{1,5},{5,1},{2,6},{6,2},{3,7},{7,3},{8,12},{12,8},{9,1... | collective-permute-start | bytes 860168 | tf_op jit(solution)/shard_map/ppermute | solution.py:217
  30.0 6.5 %collective-permute-done = bf16[1120,128]{1,0:T(8,128)(2,1)S(1)} collective-permute-done((bf16[1120,128]{1,0:T(8,128)(2,1)S(1)}, bf16[1120,128]{1,0:T(8,128)(2,1)S(1)}, u32[]{:S(2)}, u32[]{:S(2)}) %collective-permute-start) | collective-permute-done | bytes 286752 | tf_op jit(solution)/shard_map/ppermute | solution.py:217
  36.4 0.1 pad_maximum_fusion.b00_ref
  36.5 3.4 %collective-permute-start.2 = (bf16[2,1120,128]{2,1,0:T(8,128)(2,1)S(1)}, bf16[2,1120,128]{2,1,0:T(8,128)(2,1)S(1)}, u32[]{:S(2)}, u32[]{:S(2)}) collective-permute-start(bf16[2,1120,128]{2,1,0:T(8,128)(2,1)S(1)} %pad_maximum_fusion.b00_ref), channel_id=1, source_target_pairs={{0,256},{256,0},{1,257},{257,1},{2,258},{258,2},{3,259},{259,3},{4... | collective-permute-start | bytes 1720328 | tf_op jit(solution)/shard_map/ppermute | solution.py:217
  39.9 0.0 all-to-all-done
  39.9 0.1 broadcast_in_dim.30
  40.0 1.1 %broadcast_in_dim.31 = bf16[4,32,4224]{2,1,0:T(8,128)(2,1)} broadcast(bf16[32,4224]{1,0:T(8,128)(2,1)S(1)} %broadcast_in_dim.30), dimensions={1,2} | broadcast | bytes 1351680 | tf_op jit(solution)/shard_map/broadcast_in_dim | solution.py:231
  41.1 4.9 %all-to-all-start.1 = ((bf16[4,32,4224]{2,1,0:T(8,128)(2,1)}), bf16[4,32,4224]{2,1,0:T(8,128)(2,1)S(1)}, u32[]{:S(2)}, u32[]{:S(2)}) async-start(bf16[4,32,4224]{2,1,0:T(8,128)(2,1)} %broadcast_in_dim.31), calls=%async_computation.1 | async-start | bytes 2162688 | tf_op jit(solution)/shard_map/all_to_all | solution.py:232
  46.0 1.9 %collective-permute-start.1 = (bf16[2,1120,128]{2,1,0:T(8,128)(2,1)S(1)}, bf16[2,1120,128]{2,1,0:T(8,128)(2,1)S(1)}, u32[]{:S(2)}, u32[]{:S(2)}) collective-permute-start(bf16[2,1120,128]{2,1,0:T(8,128)(2,1)S(1)} %pad_maximum_fusion.b00_ref), channel_id=1, source_target_pairs={{0,8},{8,0},{1,9},{9,1},{2,10},{10,2},{3,11},{11,3},{4,12},{12,4},... | collective-permute-start | bytes 1720328 | tf_op jit(solution)/shard_map/ppermute | solution.py:217
  47.9 3.7 %collective-permute-done.2.b10_ref = bf16[2,1120,128]{2,1,0:T(8,128)(2,1)S(1)} collective-permute-done((bf16[2,1120,128]{2,1,0:T(8,128)(2,1)S(1)}, bf16[2,1120,128]{2,1,0:T(8,128)(2,1)S(1)}, u32[]{:S(2)}, u32[]{:S(2)}) %collective-permute-start.2) | collective-permute-done | bytes 573472 | tf_op jit(solution)/shard_map/ppermute | solution.py:217
  51.6 1.9 %collective-permute-start.3 = (bf16[2,1120,128]{2,1,0:T(8,128)(2,1)S(1)}, bf16[2,1120,128]{2,1,0:T(8,128)(2,1)S(1)}, u32[]{:S(2)}, u32[]{:S(2)}) collective-permute-start(bf16[2,1120,128]{2,1,0:T(8,128)(2,1)S(1)} %collective-permute-done.2.b10_ref), channel_id=1, source_target_pairs={{0,8},{8,0},{1,9},{9,1},{2,10},{10,2},{3,11},{11,3},{4,12},{12,4},... | collective-permute-start | bytes 1720328 | tf_op jit(solution)/shard_map/ppermute | solution.py:217
  53.6 0.1 select_reduce_fusion
  53.7 0.1 copy.9.label_ref
  53.8 0.0 collective-permute-done.1.b01_ref
  53.8 1.7 %collective-permute-done.3.b11_ref = bf16[2,1120,128]{2,1,0:T(8,128)(2,1)S(1)} collective-permute-done((bf16[2,1120,128]{2,1,0:T(8,128)(2,1)S(1)}, bf16[2,1120,128]{2,1,0:T(8,128)(2,1)S(1)}, u32[]{:S(2)}, u32[]{:S(2)}) %collective-permute-start.3) | collective-permute-done | bytes 573472 | tf_op jit(solution)/shard_map/ppermute | solution.py:217
  55.5 2.7 %all-to-all-done.1 = bf16[4,32,4224]{2,1,0:T(8,128)(2,1)S(1)} async-done(((bf16[4,32,4224]{2,1,0:T(8,128)(2,1)}), bf16[4,32,4224]{2,1,0:T(8,128)(2,1)S(1)}, u32[]{:S(2)}, u32[]{:S(2)}) %all-to-all-start.1) | async-done | bytes 1081376 | tf_op jit(solution)/shard_map/all_to_all | solution.py:232
  58.2 1.3 %shard_map.48 = f32[16,2,8,128]{3,2,1,0:T(8,128)S(1)} custom-call(s32[5]{0:T(128)S(1)} %stack.32.place_ref, s32[4]{0:T(128)S(1)} %copy-done.1, s32[128,1]{1,0:T(8,128)S(1)} %copy.9.label_ref, bf16[128,4224]{1,0:T(8,128)(2,1)S(1)} %bitcast.19, bf16[2,1120,128]{2,1,0:T(8,128)(2,1)S(1)} %pad_maximum_fusion.b00_ref, ...), custom_call_target="tpu_custom_call" | custom-call | tf_op jit(solution)/shard_map/pallas_call | solution.py:196
  59.5 24.2 %all_to_all.15 = f32[32,8,128]{2,1,0:T(8,128)S(1)} all-to-all(f32[32,8,128]{2,1,0:T(8,128)S(1)} %bitcast.22), channel_id=1, replica_groups=mesh['xl'=2,'z'=16,'co'=2,'xh'=2,'y'=4] {'z','xh'}, dimensions={0} | all-to-all | bytes 262144 | tf_op jit(solution)/shard_map/all_to_all | solution.py:236
  83.7 0.6 reduce_sum.29
  (2 shorter events, 0.0 us)
Async XLA Ops:
  0.0 2.3 %copy-start.1 = (s32[4]{0:T(128)S(1)}, s32[4]{0:T(128)}, u32[]{:S(2)}) copy-start(s32[4]{0:T(128)} %size_ref.5) | copy-start | bytes 52
  0.0 2.3 %copy-start.2 = (s32[50]{0:T(128)S(1)}, s32[50]{0:T(128)}, u32[]{:S(2)}) copy-start(s32[50]{0:T(128)} %occ_ref.1) | copy-start | bytes 604
  2.2 22.0 %copy-start = (bf16[2500,128]{1,0:T(8,128)(2,1)S(1)}, bf16[2500,128]{1,0:T(8,128)(2,1)}, u32[]{:S(2)}) copy-start(bf16[2500,128]{1,0:T(8,128)(2,1)} %b_ref) | copy-start | bytes 1920004
  5.3 34.6 %all-to-all-start = ((bf16[16,2,4224]{2,1,0:T(2,128)(2,1)}), bf16[16,2,4224]{2,1,0:T(2,128)(2,1)S(1)}, u32[]{:S(2)}, u32[]{:S(2)}) async-start(bf16[16,2,4224]{2,1,0:T(2,128)(2,1)} %bitcast.8), calls=%async_computation | async-start | bytes 540672 | tf_op jit(solution)/shard_map/all_to_all | solution.py:225
  25.0 11.4 %collective-permute-start = (bf16[1120,128]{1,0:T(8,128)(2,1)S(1)}, bf16[1120,128]{1,0:T(8,128)(2,1)S(1)}, u32[]{:S(2)}, u32[]{:S(2)}) collective-permute-start(bf16[1120,128]{1,0:T(8,128)(2,1)S(1)} %shard_map.47), channel_id=1, source_target_pairs={{0,4},{4,0},{1,5},{5,1},{2,6},{6,2},{3,7},{7,3},{8,12},{12,8},{9,1... | collective-permute-start | bytes 860168 | tf_op jit(solution)/shard_map/ppermute | solution.py:217
  36.5 15.1 %collective-permute-start.2 = (bf16[2,1120,128]{2,1,0:T(8,128)(2,1)S(1)}, bf16[2,1120,128]{2,1,0:T(8,128)(2,1)S(1)}, u32[]{:S(2)}, u32[]{:S(2)}) collective-permute-start(bf16[2,1120,128]{2,1,0:T(8,128)(2,1)S(1)} %pad_maximum_fusion.b00_ref), channel_id=1, source_target_pairs={{0,256},{256,0},{1,257},{257,1},{2,258},{258,2},{3,259},{259,3},{4... | collective-permute-start | bytes 1720328 | tf_op jit(solution)/shard_map/ppermute | solution.py:217
  41.1 17.1 %all-to-all-start.1 = ((bf16[4,32,4224]{2,1,0:T(8,128)(2,1)}), bf16[4,32,4224]{2,1,0:T(8,128)(2,1)S(1)}, u32[]{:S(2)}, u32[]{:S(2)}) async-start(bf16[4,32,4224]{2,1,0:T(8,128)(2,1)} %broadcast_in_dim.31), calls=%async_computation.1 | async-start | bytes 2162688 | tf_op jit(solution)/shard_map/all_to_all | solution.py:232
  46.0 7.8 %collective-permute-start.1 = (bf16[2,1120,128]{2,1,0:T(8,128)(2,1)S(1)}, bf16[2,1120,128]{2,1,0:T(8,128)(2,1)S(1)}, u32[]{:S(2)}, u32[]{:S(2)}) collective-permute-start(bf16[2,1120,128]{2,1,0:T(8,128)(2,1)S(1)} %pad_maximum_fusion.b00_ref), channel_id=1, source_target_pairs={{0,8},{8,0},{1,9},{9,1},{2,10},{10,2},{3,11},{11,3},{4,12},{12,4},... | collective-permute-start | bytes 1720328 | tf_op jit(solution)/shard_map/ppermute | solution.py:217
  51.6 3.9 %collective-permute-start.3 = (bf16[2,1120,128]{2,1,0:T(8,128)(2,1)S(1)}, bf16[2,1120,128]{2,1,0:T(8,128)(2,1)S(1)}, u32[]{:S(2)}, u32[]{:S(2)}) collective-permute-start(bf16[2,1120,128]{2,1,0:T(8,128)(2,1)S(1)} %collective-permute-done.2.b10_ref), channel_id=1, source_target_pairs={{0,8},{8,0},{1,9},{9,1},{2,10},{10,2},{3,11},{11,3},{4,12},{12,4},... | collective-permute-start | bytes 1720328 | tf_op jit(solution)/shard_map/ppermute | solution.py:217
